TPU v7x, 32 devices: a whole 2x2x4 slice. The times are simulated.
32 devices in a mesh: groups: 2 (over x), expert: 16 (over z, y, core).
Axes of the slice: x: 2, y: 2, z: 4, core: 2. Of those that a mesh axis runs over, the one named last changes fastest.
Arguments:
- residual: bfloat16 [1024, 2880], P(('groups', 'expert')), parts along dimension 0, may hold values from -6 to 6
- norm_gain: float32 [2880], replicated, may hold values from 0.1 to 1.9
- expert_ids: int32 [1024, 4], P(('groups', 'expert')), parts along dimension 0, may hold values from 0 to 7, all different within a row; in each aligned block of 32 rows (0 to 31, 32 to 63, ...) at most 32 rows name the same one
- route_logits: float32 [1024, 4], P(('groups', 'expert')), parts along dimension 0, may hold values from -6 to 6
- w_gate_up: bfloat16 [16, 2880, 1536], P('expert'), may hold values from -0.109375 to 0.109375
- w_down: bfloat16 [16, 768, 2880], P('expert'), may hold values from -0.15625 to 0.15625
Outputs:
- layer_out: bfloat16 [1024, 2880], P(('groups', 'expert')), parts along dimension 0
There are 2 independent parts, one for each index of `groups`. A program takes and returns all parts, laid end to end along the dimension named above; an argument that names none is the same for every part. Nothing has to cross between parts.
Inputs may be any that keep to these rules, and one draw needn't show every extreme that they name: `expert_ids`: in each aligned block of 32 tokens no expert is named by more than 32 routes, and some expert reaches 32 in some block; the 4 experts of a token differ.
All inputs are finite; a program needn't handle non-finite values.
Results may differ from a plain program's by a relative error of at most 0.0062.
Values may be sent and summed in bfloat16 or wider, within the bound.
No kernel may reach another device: no remote copies, remote signals or barrier semaphores. Data moves between devices by JAX's collectives and lax.ppermute only.
A program may use at most 64 MiB of HBM per device.

v0:
```python
import jax
import jax.numpy as jnp
from jax import lax
from jax.sharding import PartitionSpec as P

TOP = 4


def rms_scale(hidden, gain):
    values = hidden.astype(jnp.float32)
    meansq = jnp.mean(values * values, axis=-1, keepdims=True)
    return (values * lax.rsqrt(meansq + 1e-05) * gain).astype(jnp.bfloat16)


def expert_rows(inputs, w_up, w_dn):
    shape_in = inputs.shape
    flat_rows = inputs.reshape(-1, shape_in[-1])
    half_units = w_dn.shape[0]
    projected = jnp.dot(flat_rows, w_up, preferred_element_type=jnp.float32)
    gate_part = projected[:, :half_units]
    up_part = projected[:, half_units:]
    activated = (gate_part * jax.nn.sigmoid(1.702 * gate_part) * (up_part + 1.0)).astype(
        jnp.bfloat16
    )
    output = jnp.dot(activated, w_dn, preferred_element_type=jnp.float32).astype(jnp.bfloat16)
    return output.reshape(shape_in)


def local(residual, norm_gain, expert_ids, route_logits, w_gate_up, w_down):
    tok_count = residual.shape[0]
    width = residual.shape[1]
    devices = lax.axis_size("expert")
    num_experts = devices // 2
    capacity = 2 * tok_count * TOP // num_experts
    normed = rms_scale(residual, norm_gain)
    route_weights = jax.nn.softmax(route_logits, axis=-1)
    flat_ids = expert_ids.reshape(-1)
    onehot = (flat_ids[:, None] == jnp.arange(num_experts, dtype=jnp.int32)[None, :]).astype(
        jnp.int32
    )
    before = jnp.cumsum(onehot, axis=0) - onehot
    slots = jnp.sum(before * onehot, axis=1)
    routed = jnp.repeat(normed, TOP, axis=0)
    buffer = jnp.zeros((num_experts, capacity, width), jnp.bfloat16).at[flat_ids, slots].set(routed)
    w_up_local = w_gate_up[0]
    w_dn_local = w_down[0]
    outgoing = jnp.repeat(buffer, 2, axis=0)
    partials = expert_rows(
        lax.all_to_all(outgoing, "expert", split_axis=0, concat_axis=0, tiled=True),
        w_up_local,
        w_dn_local,
    )
    returned = lax.all_to_all(partials, "expert", split_axis=0, concat_axis=0, tiled=True)
    results = jnp.sum(
        returned.reshape(num_experts, 2, capacity, width).astype(jnp.float32), axis=1
    ).astype(jnp.bfloat16)
    picked = results[flat_ids, slots].astype(jnp.float32).reshape(tok_count, TOP, width)
    combined = jnp.sum(picked * route_weights[..., None], axis=1)
    return (residual.astype(jnp.float32) + combined).astype(jnp.bfloat16)


def solution(mesh):
    placed = (
        P(("groups", "expert"), None),
        P(),
        P(("groups", "expert"), None),
        P(("groups", "expert"), None),
        P("expert", None, None),
        P("expert", None, None),
    )
    return jax.shard_map(
        local, mesh=mesh, in_specs=placed, out_specs=P(("groups", "expert"), None), check_vma=False
    )
```

profile of v0, /device:TPU:13, one launch (start us, length us, event | category | flops | bytes accessed | tf_op | source)
XLA Modules:
  0.0 187.1 jit_solution(2411712822318538205)
XLA Ops:
  0.0 0.8 copy.10
  0.8 0.1 eq.15
  0.9 0.1 reshape.76
  1.1 0.2 reduce_window_sum.11
  1.2 0.2 select_reduce_fusion
  1.4 1.1 fusion.8
  2.5 1.0 fusion.10
  3.6 0.2 broadcast_in_dim.7
  3.8 0.4 reshape.91
  4.1 0.1 broadcast_in_dim.6
  4.3 15.6 %scatter_fusion = bf16[8,32,2880]{2,1,0:T(8,128)(2,1)S(1)} fusion(bf16[8,32,2880]{2,1,0:T(8,128)(2,1)S(1)} %broadcast_in_dim.6, s32[128]{0:T(128)S(1)} %get-tuple-element.5, bf16[128,2880]{1,0:T(8,128)(2,1)S(1)} %reshape.91), kind=kCustom, calls=%fused_computation.1 | custom fusion | bytes 2212864 | tf_op jit(solution)/shard_map/scatter | solution.py:44
  19.8 0.3 broadcast_in_dim.8
  20.1 73.6 %all_to_all.10 = bf16[16,32,2880]{2,1,0:T(8,128)(2,1)S(1)} all-to-all(bf16[16,32,2880]{2,1,0:T(8,128)(2,1)S(1)} %bitcast.22), channel_id=1, replica_groups=mesh['groups'=2,'expert'=16] {'expert'}, dimensions={0} | all-to-all | bytes 5898240 | tf_op jit(solution)/shard_map/all_to_all | solution.py:49
  93.7 7.5 %fusion = f32[512,1536]{1,0:T(8,128)S(1)} fusion(bf16[512,2880]{1,0:T(8,128)(2,1)S(1)} %bitcast.24, bf16[1,2880,1536]{2,1,0:T(8,128)(2,1)} %param.10), kind=kOutput, calls=%fused_computation.2 | convolution fusion | flops 4529848320 | bytes 14942208 | tf_op jit(solution)/shard_map/dot_general | solution.py:19
  101.3 2.6 %convolution_convert_fusion = bf16[512,2880]{0,1:T(8,128)(2,1)S(1)} fusion(bf16[1,768,2880]{1,2,0:T(8,128)(2,1)S(1)} %bitcast.26, f32[512,1536]{1,0:T(8,128)S(1)} %fusion), kind=kOutput, calls=%fused_computation.4 | convolution fusion | flops 2269544448 | bytes 10518528 | tf_op jit(solution)/shard_map/dot_general | solution.py:25
  103.9 3.0 %copy.12 = bf16[512,2880]{1,0:T(8,128)(2,1)} copy(bf16[512,2880]{0,1:T(8,128)(2,1)S(1)} %convolution_convert_fusion) | data formatting | bytes 5898240 | tf_op jit(solution)/shard_map/convert_element_type | solution.py:25
  106.9 5.3 %all-to-all-start.1 = ((bf16[16,32,2880]{2,1,0:T(8,128)(2,1)}), bf16[16,32,2880]{2,1,0:T(8,128)(2,1)}, u32[]{:S(2)}, u32[]{:S(2)}) async-start(bf16[16,32,2880]{2,1,0:T(8,128)(2,1)} %bitcast.6), calls=%async_computation.1 | async-start | bytes 6029312 | tf_op jit(solution)/shard_map/all_to_all | solution.py:53
  112.3 0.1 copy.13
  112.4 67.0 %all-to-all-done.1 = bf16[16,32,2880]{2,1,0:T(8,128)(2,1)} async-done(((bf16[16,32,2880]{2,1,0:T(8,128)(2,1)}), bf16[16,32,2880]{2,1,0:T(8,128)(2,1)}, u32[]{:S(2)}, u32[]{:S(2)}) %all-to-all-start.1) | async-done | bytes 2949152 | tf_op jit(solution)/shard_map/all_to_all | solution.py:53
  179.4 2.4 %bitcast_reduce_fusion = bf16[8,32,2880]{2,1,0:T(8,128)(2,1)S(1)} fusion(bf16[16,32,2880]{2,1,0:T(8,128)(2,1)} %all-to-all-done.1), kind=kLoop, calls=%fused_computation.6 | loop fusion | flops 737280 | bytes 4423680 | tf_op jit(solution)/shard_map/reduce_sum | solution.py:54
  181.8 3.1 %gather_fusion = bf16[128,2880]{1,0:T(8,128)(2,1)S(1)} fusion(bf16[8,32,2880]{2,1,0:T(8,128)(2,1)S(1)} %bitcast_reduce_fusion, s32[128]{0:T(128)S(1)} %bitcast.23), kind=kCustom, calls=%fused_computation | custom fusion | bytes 1475584 | tf_op jit(solution)/shard_map/gather | solution.py:57
  184.9 0.4 reshape.82
  185.3 1.0 multiply_reduce_fusion
  186.3 0.7 fusion.11
  (15 shorter events, 0.2 us)
Async XLA Ops:
  20.1 81.1 %slice-start = ((s8[4423680]{0:T(1024)(128)(4,1)}), s8[4194304]{0:T(1024)(128)(4,1)S(1)}, s32[]{:S(2)}) async-start(s8[4423680]{0:T(1024)(128)(4,1)} %bitcast.25), calls=%async_computation.2 | async-start | bytes 8388608
  93.7 7.5 %slice-start.1 = ((s8[4423680]{0:T(1024)(128)(4,1)}), s8[229376]{0:T(1024)(128)(4,1)S(1)}, s32[]{:S(2)}) async-start(s8[4423680]{0:T(1024)(128)(4,1)} %bitcast.25), calls=%async_computation.3 | async-start | bytes 458752
  106.9 5.3 %copy-start.1 = (f32[32,4]{0,1:T(4,128)S(1)}, f32[32,4]{0,1:T(4,128)}, u32[]{:S(2)}) copy-start(f32[32,4]{0,1:T(4,128)} %param.9) | copy-start | bytes 1540
  106.9 72.5 %all-to-all-start.1 = ((bf16[16,32,2880]{2,1,0:T(8,128)(2,1)}), bf16[16,32,2880]{2,1,0:T(8,128)(2,1)}, u32[]{:S(2)}, u32[]{:S(2)}) async-start(bf16[16,32,2880]{2,1,0:T(8,128)(2,1)} %bitcast.6), calls=%async_computation.1 | async-start | bytes 6029312 | tf_op jit(solution)/shard_map/all_to_all | solution.py:53
  184.9 1.4 copy-start
where the time goes:
time: 187 us
  blocking collectives  73.6 us (39%)
  waiting for transfers between devices  67 us (36%)
  local copies, waits for them, and re-layouts  24 us (13%)
  matrix products  10.1 us (5%)
  other arithmetic  6.79 us (4%)
  starting transfers between devices  5.33 us (3%)
    all_to_all x1, blocking collectives, local(): lax.all_to_all(outgoing, 'expert', split_axis=0, concat_axis=0, tiled=True)  73.6 us
    all_to_all x1, waiting for transfers between devices, local(): lax.all_to_all(partials, 'expert', split_axis=0, concat_axis=0, tiled=True)  67 us
    scatter x1, local copies, waits for them, and re-layouts, local(): jnp.zeros((num_experts, capacity, width), jnp.bfloat16).at[flat_ids, slots]  15.6 us
    dot_general x1, matrix products, expert_rows(): projected = jnp.dot(flat_rows, w_up, preferred_element_type=jnp.float32)  7.52 us
    all_to_all x1, starting transfers between devices, local(): lax.all_to_all(partials, 'expert', split_axis=0, concat_axis=0, tiled=True)  5.33 us
  transfers between devices with their start and end apart: 1, of which 1 were waited for; matrix products, arithmetic and copies ran while one was open for 0% of the time, Pallas kernels for 0%

commit v1 on v0

v1 whole, which is shorter than its diff:
```python
import jax
import jax.numpy as jnp
from jax import lax
from jax.sharding import PartitionSpec as P

LANES = 128


def rms_scale(hidden, gain):
    values = hidden.astype(jnp.float32)
    meansq = jnp.mean(values * values, axis=-1, keepdims=True)
    return (values * lax.rsqrt(meansq + 1e-05) * gain).astype(jnp.bfloat16)


def swap(x, mask):
    n = lax.axis_size("expert")
    return lax.ppermute(x, "expert", [(i, i ^ mask) for i in range(n)])


def gather_blocks(own):
    n = lax.axis_size("expert")
    blocks = {0: own}
    if n == 16:
        blocks[4] = swap(own, 4)
        blocks[12] = swap(own, 12)
        blocks[2] = swap(own, 2)
        blocks[6] = swap(blocks[4], 2)
        blocks[8] = swap(blocks[12], 4)
        blocks[14] = swap(blocks[12], 2)
        blocks[10] = swap(blocks[8], 2)
    else:
        mask = n // 2
        while mask > 1:
            for r in list(blocks):
                blocks[r ^ mask] = swap(blocks[r], mask)
            mask //= 2
    for r in list(blocks):
        blocks[r ^ 1] = swap(blocks[r], 1)
    return blocks


def add(*terms):
    total = terms[0].astype(jnp.float32)
    for term in terms[1:]:
        total = total + term.astype(jnp.float32)
    return total.astype(jnp.bfloat16)


def scatter_sum(parts):
    n = lax.axis_size("expert")
    parts = {r: add(parts[r], swap(parts[r ^ 1], 1)) for r in parts if not r & 1}
    if n == 16:
        parts = {r: add(parts[r], swap(parts[r ^ 2], 2)) for r in (8, 12, 4, 0)}
        far = add(parts[12], swap(parts[8], 4))
        return parts[0], swap(parts[4], 4), swap(far, 12)
    mask = 2
    while mask < n:
        parts = {r: add(parts[r], swap(parts[r ^ mask], mask)) for r in parts if not r & mask}
        mask *= 2
    return (parts[0],)


def local(residual, norm_gain, expert_ids, route_logits, w_gate_up, w_down):
    tokens, width = residual.shape
    n = lax.axis_size("expert")
    experts = n // 2
    half_units = w_down.shape[1]
    normed = rms_scale(residual, norm_gain)
    route_weights = jax.nn.softmax(route_logits, axis=-1)
    named = expert_ids[:, :, None] == jnp.arange(experts, dtype=jnp.int32)
    by_expert = jnp.sum(jnp.where(named, route_weights[:, :, None], 0.0), axis=1)
    high = by_expert.astype(jnp.bfloat16)
    low = (by_expert - high.astype(jnp.float32)).astype(jnp.bfloat16)
    filler = -(width + 2 * experts) % LANES
    own = jnp.concatenate([normed, high, low, jnp.zeros((tokens, filler), jnp.bfloat16)], axis=1)

    blocks = gather_blocks(own)
    order = sorted(blocks)
    rows = jnp.concatenate([blocks[r] for r in order], axis=0)
    mine = lax.axis_index("expert") // 2
    column = jnp.arange(2 * experts, dtype=jnp.int32) % experts
    tail = rows[:, width : width + 2 * experts].astype(jnp.float32)
    weight = jnp.sum(jnp.where(column == mine, tail, 0.0), axis=1, keepdims=True)
    projected = jnp.dot(rows[:, :width], w_gate_up[0], preferred_element_type=jnp.float32)
    a = projected[:, :half_units]
    b = projected[:, half_units:]
    act = (a * jax.nn.sigmoid(1.702 * a) * (b + 1.0) * weight).astype(jnp.bfloat16)
    out = jnp.dot(act, w_down[0], preferred_element_type=jnp.float32).astype(jnp.bfloat16)
    parts = {r: out[k * tokens : (k + 1) * tokens] for k, r in enumerate(order)}
    return add(residual, *scatter_sum(parts))


def solution(mesh):
    placed = (
        P(("groups", "expert"), None),
        P(),
        P(("groups", "expert"), None),
        P(("groups", "expert"), None),
        P("expert", None, None),
        P("expert", None, None),
    )
    return jax.shard_map(
        local, mesh=mesh, in_specs=placed, out_specs=P(("groups", "expert"), None), check_vma=False
    )
```

time: 187 us -> 86.2 us (0.46)
  the two profiles are of different devices: /device:TPU:13 before, /device:TPU:0 now
where the time goes in v1:
time: 86.2 us; the launch traced here: 86 us
  waiting for transfers between devices  36.2 us (42%)
  starting transfers between devices  19 us (22%)
  matrix products  11.8 us (14%)
  local copies, waits for them, and re-layouts  11.4 us (13%)
  other arithmetic  7.29 us (8%)
    ppermute x30, waiting for transfers between devices, swap(): return lax.ppermute(x, 'expert', [(i, i ^ mask) for i in range(n)])  36.2 us
    ppermute x30, starting transfers between devices, swap(): return lax.ppermute(x, 'expert', [(i, i ^ mask) for i in range(n)])  19 us
    unnamed x21, local copies, waits for them, and re-layouts  10.4 us
    dot_general x1, matrix products, local(): jnp.dot(rows[:, :width], w_gate_up[0], preferred_element_type=jnp.float32)  8.47 us
    dot_general x1, matrix products, local(): jnp.dot(act, w_down[0], preferred_element_type=jnp.float32)  3.38 us
  transfers between devices with their start and end apart: 30, of which 12 were waited for; matrix products, arithmetic and copies ran while one was open for 13% of the time, Pallas kernels for 0%

profile of v1, /device:TPU:0, one launch (start us, length us, event | category | flops | bytes accessed | tf_op | source)
XLA Modules:
  0.0 86.0 jit_solution(246912983979532931)
XLA Ops:
  0.7 0.7 fusion.18
  3.0 1.1 %fusion.11 = f32[32]{0:T(128)S(1)} fusion(bf16[32,2880]{1,0:T(8,128)(2,1)} %param.6), kind=kLoop, calls=%fused_computation.15 | loop fusion | flops 276448 | bytes 184448 | tf_op jit(solution)/shard_map/reduce_sum | solution.py:11
  4.1 1.0 %fusion.13 = bf16[32,2880]{1,0:T(8,128)(2,1)S(1)} fusion(bf16[32,2880]{1,0:T(8,128)(2,1)} %param.6, f32[2880]{0:T(1024)} %param.7, f32[32]{0:T(128)S(1)} %add_rsqrt_fusion), kind=kLoop, calls=%fused_computation.17 | loop fusion | flops 368640 | bytes 380288 | tf_op jit(solution)/shard_map/convert_element_type | solution.py:12
  5.7 2.6 %collective-permute-start.1 = (bf16[32,2944]{1,0:T(8,128)(2,1)S(1)}, bf16[32,2944]{1,0:T(8,128)(2,1)S(1)}, u32[]{:S(2)}, u32[]{:S(2)}) collective-permute-start(bf16[32,2944]{1,0:T(8,128)(2,1)S(1)} %concatenate.6), channel_id=1, source_target_pairs={{0,2},{1,3},{2,0},{3,1},{4,6},{5,7},{6,4},{7,5},{8,10},{9,11},{10,... | collective-permute-start | bytes 565256 | tf_op jit(solution)/shard_map/ppermute | solution.py:17
  8.3 1.6 %collective-permute-start.3 = (bf16[32,2944]{1,0:T(8,128)(2,1)S(1)}, bf16[32,2944]{1,0:T(8,128)(2,1)S(1)}, u32[]{:S(2)}, u32[]{:S(2)}) collective-permute-start(bf16[32,2944]{1,0:T(8,128)(2,1)S(1)} %concatenate.6), channel_id=1, source_target_pairs={{0,4},{1,5},{2,6},{3,7},{4,0},{5,1},{6,2},{7,3},{8,12},{9,13},{10,... | collective-permute-start | bytes 565256 | tf_op jit(solution)/shard_map/ppermute | solution.py:17
  9.9 2.5 %collective-permute-start.7 = (bf16[32,2944]{1,0:T(8,128)(2,1)S(1)}, bf16[32,2944]{1,0:T(8,128)(2,1)S(1)}, u32[]{:S(2)}, u32[]{:S(2)}) collective-permute-start(bf16[32,2944]{1,0:T(8,128)(2,1)S(1)} %concatenate.6), channel_id=1, source_target_pairs={{0,12},{1,13},{2,14},{3,15},{4,8},{5,9},{6,10},{7,11},{8,4},{9,5},... | collective-permute-start | bytes 565256 | tf_op jit(solution)/shard_map/ppermute | solution.py:17
  13.1 2.0 %collective-permute-done.3 = bf16[32,2944]{1,0:T(8,128)(2,1)S(1)} collective-permute-done((bf16[32,2944]{1,0:T(8,128)(2,1)S(1)}, bf16[32,2944]{1,0:T(8,128)(2,1)S(1)}, u32[]{:S(2)}, u32[]{:S(2)}) %collective-permute-start.3) | collective-permute-done | bytes 188448 | tf_op jit(solution)/shard_map/ppermute | solution.py:17
  15.5 5.8 %collective-permute-done.7 = bf16[32,2944]{1,0:T(8,128)(2,1)S(1)} collective-permute-done((bf16[32,2944]{1,0:T(8,128)(2,1)S(1)}, bf16[32,2944]{1,0:T(8,128)(2,1)S(1)}, u32[]{:S(2)}, u32[]{:S(2)}) %collective-permute-start.7) | collective-permute-done | bytes 188448 | tf_op jit(solution)/shard_map/ppermute | solution.py:17
  24.3 2.9 %collective-permute-done.8 = bf16[32,2944]{1,0:T(8,128)(2,1)S(1)} collective-permute-done((bf16[32,2944]{1,0:T(8,128)(2,1)S(1)}, bf16[32,2944]{1,0:T(8,128)(2,1)S(1)}, u32[]{:S(2)}, u32[]{:S(2)}) %collective-permute-start.8) | collective-permute-done | bytes 188448 | tf_op jit(solution)/shard_map/ppermute | solution.py:17
  29.3 1.1 %collective-permute-done.13 = bf16[32,2944]{1,0:T(8,128)(2,1)S(1)} collective-permute-done((bf16[32,2944]{1,0:T(8,128)(2,1)S(1)}, bf16[32,2944]{1,0:T(8,128)(2,1)S(1)}, u32[]{:S(2)}, u32[]{:S(2)}) %collective-permute-start.13) | collective-permute-done | bytes 188448 | tf_op jit(solution)/shard_map/ppermute | solution.py:17
  30.5 0.7 constant_dynamic-update-slice_fusion.10
  31.9 3.9 %collective-permute-done.10 = bf16[32,2944]{1,0:T(8,128)(2,1)S(1)} collective-permute-done((bf16[32,2944]{1,0:T(8,128)(2,1)S(1)}, bf16[32,2944]{1,0:T(8,128)(2,1)S(1)}, u32[]{:S(2)}, u32[]{:S(2)}) %collective-permute-start.10) | collective-permute-done | bytes 188448 | tf_op jit(solution)/shard_map/ppermute | solution.py:17
  37.1 0.7 constant_dynamic-update-slice_fusion.6
  42.0 8.5 %fusion = f32[512,1536]{1,0:T(8,128)S(1)} fusion(bf16[1,2880,1536]{2,1,0:T(8,128)(2,1)} %param.10, bf16[512,2944]{1,0:T(8,128)(2,1)} %constant_dynamic-update-slice_fusion), kind=kOutput, calls=%fused_computation | convolution fusion | flops 4529848320 | bytes 15007744 | tf_op jit(solution)/shard_map/dot_general | solution.py:84
  50.4 1.1 %select_reduce_fusion = f32[512]{0:T(512)S(1)} fusion(bf16[512,2944]{1,0:T(8,128)(2,1)} %constant_dynamic-update-slice_fusion, pred[16]{0:T(512)(128)(4,1)S(1)} %fusion.19), kind=kLoop, calls=%fused_computation.34 | loop fusion | flops 24064 | bytes 18448 | tf_op jit(solution)/shard_map/reduce_sum | solution.py:83
  51.6 3.4 %convolution_convert_fusion = bf16[512,2880]{1,0:T(8,128)(2,1)S(1)} fusion(bf16[1,768,2880]{1,2,0:T(8,128)(2,1)S(1)} %bitcast.7, f32[512,1536]{1,0:T(8,128)S(1)} %fusion, f32[512]{0:T(512)S(1)} %select_reduce_fusion), kind=kOutput, calls=%fused_computation.2 | convolution fusion | flops 2269937664 | bytes 10520576 | tf_op jit(solution)/shard_map/dot_general | solution.py:88
  58.4 1.5 %collective-permute-start.27 = (bf16[32,2880]{1,0:T(8,128)(2,1)S(1)}, bf16[32,2880]{1,0:T(8,128)(2,1)S(1)}, u32[]{:S(2)}, u32[]{:S(2)}) collective-permute-start(bf16[32,2880]{1,0:T(8,128)(2,1)S(1)} %get-tuple-element.16), channel_id=1, source_target_pairs={{0,2},{1,3},{2,0},{3,1},{4,6},{5,7},{6,4},{7,5},{8,10},{9,11},{10,... | collective-permute-start | bytes 552968 | tf_op jit(solution)/shard_map/ppermute | solution.py:17
  60.4 5.0 %collective-permute-done.20 = bf16[32,2880]{1,0:T(8,128)(2,1)S(1)} collective-permute-done((bf16[32,2880]{1,0:T(8,128)(2,1)S(1)}, bf16[32,2880]{1,0:T(8,128)(2,1)S(1)}, u32[]{:S(2)}, u32[]{:S(2)}) %collective-permute-start.20) | collective-permute-done | bytes 184352 | tf_op jit(solution)/shard_map/ppermute | solution.py:17
  65.4 4.0 %collective-permute-done.27 = bf16[32,2880]{1,0:T(8,128)(2,1)S(1)} collective-permute-done((bf16[32,2880]{1,0:T(8,128)(2,1)S(1)}, bf16[32,2880]{1,0:T(8,128)(2,1)S(1)}, u32[]{:S(2)}, u32[]{:S(2)}) %collective-permute-start.27) | collective-permute-done | bytes 184352 | tf_op jit(solution)/shard_map/ppermute | solution.py:17
  70.5 1.7 %collective-permute-start.21 = (bf16[32,2880]{1,0:T(8,128)(2,1)S(1)}, bf16[32,2880]{1,0:T(8,128)(2,1)S(1)}, u32[]{:S(2)}, u32[]{:S(2)}) collective-permute-start(bf16[32,2880]{1,0:T(8,128)(2,1)S(1)} %get-tuple-element.19), channel_id=1, source_target_pairs={{0,4},{1,5},{2,6},{3,7},{4,0},{5,1},{6,2},{7,3},{8,12},{9,13},{10,... | collective-permute-start | bytes 552968 | tf_op jit(solution)/shard_map/ppermute | solution.py:17
  72.8 4.4 %collective-permute-done.28 = bf16[32,2880]{1,0:T(8,128)(2,1)S(1)} collective-permute-done((bf16[32,2880]{1,0:T(8,128)(2,1)S(1)}, bf16[32,2880]{1,0:T(8,128)(2,1)S(1)}, u32[]{:S(2)}, u32[]{:S(2)}) %collective-permute-start.28) | collective-permute-done | bytes 184352 | tf_op jit(solution)/shard_map/ppermute | solution.py:17
  77.3 2.0 %collective-permute-start.29 = (bf16[32,2880]{1,0:T(8,128)(2,1)S(1)}, bf16[32,2880]{1,0:T(8,128)(2,1)S(1)}, u32[]{:S(2)}, u32[]{:S(2)}) collective-permute-start(bf16[32,2880]{1,0:T(8,128)(2,1)S(1)} %add_convert_fusion), channel_id=1, source_target_pairs={{0,12},{1,13},{2,14},{3,15},{4,8},{5,9},{6,10},{7,11},{8,4},{9,5},... | collective-permute-start | bytes 552968 | tf_op jit(solution)/shard_map/ppermute | solution.py:17
  79.3 5.8 %collective-permute-done.29 = bf16[32,2880]{1,0:T(8,128)(2,1)S(1)} collective-permute-done((bf16[32,2880]{1,0:T(8,128)(2,1)S(1)}, bf16[32,2880]{1,0:T(8,128)(2,1)S(1)}, u32[]{:S(2)}, u32[]{:S(2)}) %collective-permute-start.29) | collective-permute-done | bytes 184352 | tf_op jit(solution)/shard_map/ppermute | solution.py:17
  85.1 0.8 fusion.16
  (80 shorter events, 21.0 us)
Async XLA Ops:
  5.2 16.6 %collective-permute-start = (bf16[32,2944]{1,0:T(8,128)(2,1)S(1)}, bf16[32,2944]{1,0:T(8,128)(2,1)S(1)}, u32[]{:S(2)}, u32[]{:S(2)}) collective-permute-start(bf16[32,2944]{1,0:T(8,128)(2,1)S(1)} %concatenate.6), channel_id=1, source_target_pairs={{0,1},{1,0},{2,3},{3,2},{4,5},{5,4},{6,7},{7,6},{8,9},{9,8},{10,11... | collective-permute-start | bytes 565256 | tf_op jit(solution)/shard_map/ppermute | solution.py:17
  5.7 16.1 %collective-permute-start.1 = (bf16[32,2944]{1,0:T(8,128)(2,1)S(1)}, bf16[32,2944]{1,0:T(8,128)(2,1)S(1)}, u32[]{:S(2)}, u32[]{:S(2)}) collective-permute-start(bf16[32,2944]{1,0:T(8,128)(2,1)S(1)} %concatenate.6), channel_id=1, source_target_pairs={{0,2},{1,3},{2,0},{3,1},{4,6},{5,7},{6,4},{7,5},{8,10},{9,11},{10,... | collective-permute-start | bytes 565256 | tf_op jit(solution)/shard_map/ppermute | solution.py:17
  8.3 6.8 %collective-permute-start.3 = (bf16[32,2944]{1,0:T(8,128)(2,1)S(1)}, bf16[32,2944]{1,0:T(8,128)(2,1)S(1)}, u32[]{:S(2)}, u32[]{:S(2)}) collective-permute-start(bf16[32,2944]{1,0:T(8,128)(2,1)S(1)} %concatenate.6), channel_id=1, source_target_pairs={{0,4},{1,5},{2,6},{3,7},{4,0},{5,1},{6,2},{7,3},{8,12},{9,13},{10,... | collective-permute-start | bytes 565256 | tf_op jit(solution)/shard_map/ppermute | solution.py:17
  9.9 11.4 %collective-permute-start.7 = (bf16[32,2944]{1,0:T(8,128)(2,1)S(1)}, bf16[32,2944]{1,0:T(8,128)(2,1)S(1)}, u32[]{:S(2)}, u32[]{:S(2)}) collective-permute-start(bf16[32,2944]{1,0:T(8,128)(2,1)S(1)} %concatenate.6), channel_id=1, source_target_pairs={{0,12},{1,13},{2,14},{3,15},{4,8},{5,9},{6,10},{7,11},{8,4},{9,5},... | collective-permute-start | bytes 565256 | tf_op jit(solution)/shard_map/ppermute | solution.py:17
  15.1 13.5 %collective-permute-start.4 = (bf16[32,2944]{1,0:T(8,128)(2,1)S(1)}, bf16[32,2944]{1,0:T(8,128)(2,1)S(1)}, u32[]{:S(2)}, u32[]{:S(2)}) collective-permute-start(bf16[32,2944]{1,0:T(8,128)(2,1)S(1)} %collective-permute-done.3), channel_id=1, source_target_pairs={{0,1},{1,0},{2,3},{3,2},{4,5},{5,4},{6,7},{7,6},{8,9},{9,8},{10,11... | collective-permute-start | bytes 565256 | tf_op jit(solution)/shard_map/ppermute | solution.py:17
  15.1 14.0 %collective-permute-start.5 = (bf16[32,2944]{1,0:T(8,128)(2,1)S(1)}, bf16[32,2944]{1,0:T(8,128)(2,1)S(1)}, u32[]{:S(2)}, u32[]{:S(2)}) collective-permute-start(bf16[32,2944]{1,0:T(8,128)(2,1)S(1)} %collective-permute-done.3), channel_id=1, source_target_pairs={{0,2},{1,3},{2,0},{3,1},{4,6},{5,7},{6,4},{7,5},{8,10},{9,11},{10,... | collective-permute-start | bytes 565256 | tf_op jit(solution)/shard_map/ppermute | solution.py:17
  21.3 5.9 %collective-permute-start.8 = (bf16[32,2944]{1,0:T(8,128)(2,1)S(1)}, bf16[32,2944]{1,0:T(8,128)(2,1)S(1)}, u32[]{:S(2)}, u32[]{:S(2)}) collective-permute-start(bf16[32,2944]{1,0:T(8,128)(2,1)S(1)} %collective-permute-done.7), channel_id=1, source_target_pairs={{0,4},{1,5},{2,6},{3,7},{4,0},{5,1},{6,2},{7,3},{8,12},{9,13},{10,... | collective-permute-start | bytes 565256 | tf_op jit(solution)/shard_map/ppermute | solution.py:17
  21.9 18.0 %collective-permute-start.12 = (bf16[32,2944]{1,0:T(8,128)(2,1)S(1)}, bf16[32,2944]{1,0:T(8,128)(2,1)S(1)}, u32[]{:S(2)}, u32[]{:S(2)}) collective-permute-start(bf16[32,2944]{1,0:T(8,128)(2,1)S(1)} %collective-permute-done.7), channel_id=1, source_target_pairs={{0,1},{1,0},{2,3},{3,2},{4,5},{5,4},{6,7},{7,6},{8,9},{9,8},{10,11... | collective-permute-start | bytes 565256 | tf_op jit(solution)/shard_map/ppermute | solution.py:17
  23.8 6.7 %collective-permute-start.13 = (bf16[32,2944]{1,0:T(8,128)(2,1)S(1)}, bf16[32,2944]{1,0:T(8,128)(2,1)S(1)}, u32[]{:S(2)}, u32[]{:S(2)}) collective-permute-start(bf16[32,2944]{1,0:T(8,128)(2,1)S(1)} %collective-permute-done.7), channel_id=1, source_target_pairs={{0,2},{1,3},{2,0},{3,1},{4,6},{5,7},{6,4},{7,5},{8,10},{9,11},{10,... | collective-permute-start | bytes 565256 | tf_op jit(solution)/shard_map/ppermute | solution.py:17
  27.2 9.9 %collective-permute-start.9 = (bf16[32,2944]{1,0:T(8,128)(2,1)S(1)}, bf16[32,2944]{1,0:T(8,128)(2,1)S(1)}, u32[]{:S(2)}, u32[]{:S(2)}) collective-permute-start(bf16[32,2944]{1,0:T(8,128)(2,1)S(1)} %collective-permute-done.8), channel_id=1, source_target_pairs={{0,1},{1,0},{2,3},{3,2},{4,5},{5,4},{6,7},{7,6},{8,9},{9,8},{10,11... | collective-permute-start | bytes 565256 | tf_op jit(solution)/shard_map/ppermute | solution.py:17
  28.6 7.1 %collective-permute-start.10 = (bf16[32,2944]{1,0:T(8,128)(2,1)S(1)}, bf16[32,2944]{1,0:T(8,128)(2,1)S(1)}, u32[]{:S(2)}, u32[]{:S(2)}) collective-permute-start(bf16[32,2944]{1,0:T(8,128)(2,1)S(1)} %collective-permute-done.8), channel_id=1, source_target_pairs={{0,2},{1,3},{2,0},{3,1},{4,6},{5,7},{6,4},{7,5},{8,10},{9,11},{10,... | collective-permute-start | bytes 565256 | tf_op jit(solution)/shard_map/ppermute | solution.py:17
  29.1 6.6 %collective-permute-start.6 = (bf16[32,2944]{1,0:T(8,128)(2,1)S(1)}, bf16[32,2944]{1,0:T(8,128)(2,1)S(1)}, u32[]{:S(2)}, u32[]{:S(2)}) collective-permute-start(bf16[32,2944]{1,0:T(8,128)(2,1)S(1)} %collective-permute-done.5), channel_id=1, source_target_pairs={{0,1},{1,0},{2,3},{3,2},{4,5},{5,4},{6,7},{7,6},{8,9},{9,8},{10,11... | collective-permute-start | bytes 565256 | tf_op jit(solution)/shard_map/ppermute | solution.py:17
  30.5 10.8 %collective-permute-start.14 = (bf16[32,2944]{1,0:T(8,128)(2,1)S(1)}, bf16[32,2944]{1,0:T(8,128)(2,1)S(1)}, u32[]{:S(2)}, u32[]{:S(2)}) collective-permute-start(bf16[32,2944]{1,0:T(8,128)(2,1)S(1)} %collective-permute-done.13), channel_id=1, source_target_pairs={{0,1},{1,0},{2,3},{3,2},{4,5},{5,4},{6,7},{7,6},{8,9},{9,8},{10,11... | collective-permute-start | bytes 565256 | tf_op jit(solution)/shard_map/ppermute | solution.py:17
  56.2 3.7 %collective-permute-start.18 = (bf16[32,2880]{1,0:T(8,128)(2,1)S(1)}, bf16[32,2880]{1,0:T(8,128)(2,1)S(1)}, u32[]{:S(2)}, u32[]{:S(2)}) collective-permute-start(bf16[32,2880]{1,0:T(8,128)(2,1)S(1)} %get-tuple-element.13), channel_id=1, source_target_pairs={{0,1},{1,0},{2,3},{3,2},{4,5},{5,4},{6,7},{7,6},{8,9},{9,8},{10,11... | collective-permute-start | bytes 552968 | tf_op jit(solution)/shard_map/ppermute | solution.py:17
  56.7 3.7 %collective-permute-start.25 = (bf16[32,2880]{1,0:T(8,128)(2,1)S(1)}, bf16[32,2880]{1,0:T(8,128)(2,1)S(1)}, u32[]{:S(2)}, u32[]{:S(2)}) collective-permute-start(bf16[32,2880]{1,0:T(8,128)(2,1)S(1)} %get-tuple-element.9), channel_id=1, source_target_pairs={{0,1},{1,0},{2,3},{3,2},{4,5},{5,4},{6,7},{7,6},{8,9},{9,8},{10,11... | collective-permute-start | bytes 552968 | tf_op jit(solution)/shard_map/ppermute | solution.py:17
  57.8 7.6 %collective-permute-start.20 = (bf16[32,2880]{1,0:T(8,128)(2,1)S(1)}, bf16[32,2880]{1,0:T(8,128)(2,1)S(1)}, u32[]{:S(2)}, u32[]{:S(2)}) collective-permute-start(bf16[32,2880]{1,0:T(8,128)(2,1)S(1)} %get-tuple-element.18), channel_id=1, source_target_pairs={{0,2},{1,3},{2,0},{3,1},{4,6},{5,7},{6,4},{7,5},{8,10},{9,11},{10,... | collective-permute-start | bytes 552968 | tf_op jit(solution)/shard_map/ppermute | solution.py:17
  58.4 11.1 %collective-permute-start.27 = (bf16[32,2880]{1,0:T(8,128)(2,1)S(1)}, bf16[32,2880]{1,0:T(8,128)(2,1)S(1)}, u32[]{:S(2)}, u32[]{:S(2)}) collective-permute-start(bf16[32,2880]{1,0:T(8,128)(2,1)S(1)} %get-tuple-element.16), channel_id=1, source_target_pairs={{0,2},{1,3},{2,0},{3,1},{4,6},{5,7},{6,4},{7,5},{8,10},{9,11},{10,... | collective-permute-start | bytes 552968 | tf_op jit(solution)/shard_map/ppermute | solution.py:17
  59.9 10.6 %collective-permute-start.22 = (bf16[32,2880]{1,0:T(8,128)(2,1)S(1)}, bf16[32,2880]{1,0:T(8,128)(2,1)S(1)}, u32[]{:S(2)}, u32[]{:S(2)}) collective-permute-start(bf16[32,2880]{1,0:T(8,128)(2,1)S(1)} %get-tuple-element.11), channel_id=1, source_target_pairs={{0,1},{1,0},{2,3},{3,2},{4,5},{5,4},{6,7},{7,6},{8,9},{9,8},{10,11... | collective-permute-start | bytes 552968 | tf_op jit(solution)/shard_map/ppermute | solution.py:17
  59.9 12.9 %collective-permute-start.24 = (bf16[32,2880]{1,0:T(8,128)(2,1)S(1)}, bf16[32,2880]{1,0:T(8,128)(2,1)S(1)}, u32[]{:S(2)}, u32[]{:S(2)}) collective-permute-start(bf16[32,2880]{1,0:T(8,128)(2,1)S(1)} %get-tuple-element.17), channel_id=1, source_target_pairs={{0,2},{1,3},{2,0},{3,1},{4,6},{5,7},{6,4},{7,5},{8,10},{9,11},{10,... | collective-permute-start | bytes 552968 | tf_op jit(solution)/shard_map/ppermute | solution.py:17
  69.6 7.6 %collective-permute-start.28 = (bf16[32,2880]{1,0:T(8,128)(2,1)S(1)}, bf16[32,2880]{1,0:T(8,128)(2,1)S(1)}, u32[]{:S(2)}, u32[]{:S(2)}) collective-permute-start(bf16[32,2880]{1,0:T(8,128)(2,1)S(1)} %get-tuple-element.20), channel_id=1, source_target_pairs={{0,4},{1,5},{2,6},{3,7},{4,0},{5,1},{6,2},{7,3},{8,12},{9,13},{10,... | collective-permute-start | bytes 552968 | tf_op jit(solution)/shard_map/ppermute | solution.py:17
  70.0 9.3 %collective-permute-start.15 = (bf16[32,2880]{1,0:T(8,128)(2,1)S(1)}, bf16[32,2880]{1,0:T(8,128)(2,1)S(1)}, u32[]{:S(2)}, u32[]{:S(2)}) collective-permute-start(bf16[32,2880]{1,0:T(8,128)(2,1)S(1)} %get-tuple-element.7), channel_id=1, source_target_pairs={{0,1},{1,0},{2,3},{3,2},{4,5},{5,4},{6,7},{7,6},{8,9},{9,8},{10,11... | collective-permute-start | bytes 552968 | tf_op jit(solution)/shard_map/ppermute | solution.py:17
  70.0 9.3 %collective-permute-start.17 = (bf16[32,2880]{1,0:T(8,128)(2,1)S(1)}, bf16[32,2880]{1,0:T(8,128)(2,1)S(1)}, u32[]{:S(2)}, u32[]{:S(2)}) collective-permute-start(bf16[32,2880]{1,0:T(8,128)(2,1)S(1)} %get-tuple-element.15), channel_id=1, source_target_pairs={{0,2},{1,3},{2,0},{3,1},{4,6},{5,7},{6,4},{7,5},{8,10},{9,11},{10,... | collective-permute-start | bytes 552968 | tf_op jit(solution)/shard_map/ppermute | solution.py:17
  70.5 8.8 %collective-permute-start.21 = (bf16[32,2880]{1,0:T(8,128)(2,1)S(1)}, bf16[32,2880]{1,0:T(8,128)(2,1)S(1)}, u32[]{:S(2)}, u32[]{:S(2)}) collective-permute-start(bf16[32,2880]{1,0:T(8,128)(2,1)S(1)} %get-tuple-element.19), channel_id=1, source_target_pairs={{0,4},{1,5},{2,6},{3,7},{4,0},{5,1},{6,2},{7,3},{8,12},{9,13},{10,... | collective-permute-start | bytes 552968 | tf_op jit(solution)/shard_map/ppermute | solution.py:17
  77.3 7.8 %collective-permute-start.29 = (bf16[32,2880]{1,0:T(8,128)(2,1)S(1)}, bf16[32,2880]{1,0:T(8,128)(2,1)S(1)}, u32[]{:S(2)}, u32[]{:S(2)}) collective-permute-start(bf16[32,2880]{1,0:T(8,128)(2,1)S(1)} %add_convert_fusion), channel_id=1, source_target_pairs={{0,12},{1,13},{2,14},{3,15},{4,8},{5,9},{6,10},{7,11},{8,4},{9,5},... | collective-permute-start | bytes 552968 | tf_op jit(solution)/shard_map/ppermute | solution.py:17
  (9 other events, 61.4 us)

commit v2 on v1

v2 whole, which is shorter than its diff:
```python
import functools

import jax
import jax.numpy as jnp
from jax import lax
from jax.experimental import pallas as pl
from jax.experimental.pallas import tpu as pltpu
from jax.sharding import PartitionSpec as P

LANES = 128
VMEM = pl.BlockSpec(memory_space=pltpu.VMEM)
HBM = pl.BlockSpec(memory_space=pltpu.HBM)
SMEM = pl.BlockSpec(memory_space=pltpu.SMEM)


def in_hbm(*arrays):
    return [pltpu.with_memory_space_constraint(x, pltpu.HBM) for x in arrays]


def pack_kernel(experts, _, residual_hbm, gain_hbm, ids_hbm, logits_hbm, out_ref, residual_ref, gain_ref, ids_ref, logits_ref, sems):
    copies = [
        pltpu.make_async_copy(ids_hbm, ids_ref, sems.at[0]),
        pltpu.make_async_copy(logits_hbm, logits_ref, sems.at[1]),
        pltpu.make_async_copy(residual_hbm, residual_ref, sems.at[2]),
        pltpu.make_async_copy(gain_hbm, gain_ref.at[0], sems.at[3]),
    ]
    for copy in copies:
        copy.start()
    tokens, width = residual_ref.shape
    spare = out_ref.shape[1] - width
    copies[0].wait()
    copies[1].wait()
    logits = logits_ref[...]
    grown = jnp.exp(logits - jnp.max(logits, axis=0, keepdims=True))
    weights = grown / jnp.sum(grown, axis=0, keepdims=True)
    ids = ids_ref[...]
    by_expert = jnp.concatenate(
        [jnp.sum(jnp.where(ids == e, weights, 0.0), axis=0, keepdims=True) for e in range(experts)],
        axis=0,
    )
    high = by_expert.astype(jnp.bfloat16).astype(jnp.float32)
    blank = jnp.zeros((spare - 2 * experts, tokens), jnp.float32)
    columns = jnp.concatenate([high, by_expert - high, blank], axis=0).astype(jnp.bfloat16)
    row = lax.broadcasted_iota(jnp.int32, (tokens, tokens), 0)
    eye = (row == lax.broadcasted_iota(jnp.int32, (tokens, tokens), 1)).astype(jnp.bfloat16)
    tail = lax.dot_general(
        eye, columns, (((1,), (1,)), ((), ())), preferred_element_type=jnp.float32
    ).astype(jnp.bfloat16)
    copies[2].wait()
    copies[3].wait()
    values = residual_ref[...].astype(jnp.float32)
    meansq = jnp.mean(values * values, axis=-1, keepdims=True)
    normed = (values * lax.rsqrt(meansq + 1e-05) * gain_ref[...]).astype(jnp.bfloat16)
    out_ref[...] = jnp.concatenate([normed, tail], axis=1)


def pack(mine, residual, gain, ids, logits, experts):
    tokens, width = residual.shape
    top = ids.shape[1]
    padded = -(-(width + 2 * experts) // LANES) * LANES
    return pl.pallas_call(
        functools.partial(pack_kernel, experts),
        out_shape=jax.ShapeDtypeStruct((tokens, padded), jnp.bfloat16),
        in_specs=[SMEM] + [HBM] * 4,
        out_specs=VMEM,
        scratch_shapes=[
            pltpu.VMEM((tokens, width), jnp.bfloat16),
            pltpu.VMEM((1, width), jnp.float32),
            pltpu.VMEM((top, tokens), jnp.int32),
            pltpu.VMEM((top, tokens), jnp.float32),
            pltpu.SemaphoreType.DMA((4,)),
        ],
        compiler_params=pltpu.CompilerParams(vmem_limit_bytes=8 << 20),
        name="pack",
    )(mine, *in_hbm(residual, gain, ids.T, logits.T))


def again_kernel(source, target):
    target[...] = source[...]


def again(x):
    return pl.pallas_call(
        again_kernel,
        out_shape=jax.ShapeDtypeStruct(x.shape, x.dtype),
        in_specs=[VMEM],
        out_specs=VMEM,
        compiler_params=pltpu.CompilerParams(vmem_limit_bytes=2 << 20),
        name="again",
    )(x)


def load_kernel(*refs):
    source, _, target, mark, sem = refs
    copy = pltpu.make_async_copy(source, target, sem)
    copy.start()
    mark[...] = jnp.zeros_like(mark)
    copy.wait()


def load(after, weight):
    return pl.pallas_call(
        load_kernel,
        out_shape=[
            pltpu.VMEM(weight.shape, weight.dtype),
            jax.ShapeDtypeStruct((8, LANES), jnp.float32),
        ],
        in_specs=[HBM, pl.BlockSpec(memory_space=pl.ANY)],
        out_specs=[VMEM] * 2,
        scratch_shapes=[pltpu.SemaphoreType.DMA(())],
        compiler_params=pltpu.CompilerParams(vmem_limit_bytes=1 << 20),
        cost_estimate=pl.CostEstimate(
            flops=0, bytes_accessed=2 * weight.size, transcendentals=0
        ),
        name="load",
    )(*in_hbm(weight), after)


def mlp_kernel(experts, count, mine_ref, mark_ref, *refs):
    blocks, (w_up, w_dn) = refs[:count], refs[count : count + 2]
    even_ref, odd_ref, rows, act = refs[count + 2 :]
    width, half = w_dn.shape
    tokens = even_ref.shape[1]
    views = [b.at[k] for b in blocks for k in range(b.shape[0])]
    for k, view in enumerate(views):
        rows[pl.ds(k * tokens, tokens), :] = view[...]
    tail = rows[:, width : width + 2 * experts].astype(jnp.float32)
    column = lax.rem(lax.broadcasted_iota(jnp.int32, (1, 2 * experts), 1), experts)
    weight = jnp.sum(jnp.where(column == mine_ref[0], tail, 0.0), axis=1, keepdims=True)
    x = rows[:, :width]
    step = 256 if half % 256 == 0 else half
    for at in range(0, half, step):
        a = jnp.dot(x, w_up[:, at : at + step], preferred_element_type=jnp.float32)
        b = jnp.dot(x, w_up[:, half + at : half + at + step], preferred_element_type=jnp.float32)
        act[:, at : at + step] = (a * jax.nn.sigmoid(1.702 * a) * (b + 1.0) * weight).astype(
            jnp.bfloat16
        )
    out = lax.dot_general(
        act[...], w_dn[...], (((1,), (1,)), ((), ())), preferred_element_type=jnp.float32
    ).astype(jnp.bfloat16)
    for k in range(len(views)):
        ref = (even_ref, odd_ref)[2 * k // len(views)]
        ref[k % ref.shape[0]] = out[k * tokens : (k + 1) * tokens]


def mlp(blocks, mine, mark, w_up, w_dn, experts):
    count, number, tokens = len(blocks), sum(b.shape[0] for b in blocks), blocks[0].shape[1]
    m = number * tokens
    width, half = w_dn.shape
    return pl.pallas_call(
        functools.partial(mlp_kernel, experts, count),
        out_shape=[jax.ShapeDtypeStruct((number // 2, tokens, width), jnp.bfloat16)] * 2,
        in_specs=[SMEM, pl.BlockSpec(memory_space=pl.ANY)] + [VMEM] * (count + 2),
        out_specs=[VMEM] * 2,
        scratch_shapes=[
            pltpu.VMEM((m, blocks[0].shape[2]), jnp.bfloat16),
            pltpu.VMEM((m, half), jnp.bfloat16),
        ],
        compiler_params=pltpu.CompilerParams(vmem_limit_bytes=24 << 20),
        cost_estimate=pl.CostEstimate(
            flops=6 * m * width * half, bytes_accessed=6 * width * half, transcendentals=m * half
        ),
        name="mlp",
    )(mine, mark, *blocks, *[pltpu.with_memory_space_constraint(w, pltpu.VMEM) for w in (w_up, w_dn)])


def swap(x, mask):
    n = lax.axis_size("expert")
    return lax.ppermute(x, "expert", [(i, i ^ mask) for i in range(n)])


def add(*terms):
    total = terms[0].astype(jnp.float32)
    for term in terms[1:]:
        total = total + term.astype(jnp.float32)
    return total.astype(jnp.bfloat16)


def local(residual, norm_gain, expert_ids, route_logits, w_gate_up, w_down):
    n = lax.axis_size("expert")
    tokens = residual.shape[0]
    experts = n // 2
    mine = lax.div(lax.axis_index("expert"), 2).reshape(1)
    own = pack(mine, residual, norm_gain, expert_ids, route_logits, experts)
    def terms(mixed, other):
        return mlp([mixed, other], mine, mark, w_up, w_dn, experts)

    w_dn, mark = load(own, w_down[0].T)
    if n == 16:
        together = lax.optimization_barrier
        far = swap(own, 8)
        copied = again(own)
        near = swap(copied, 4)
        side = swap(copied, 2)
        near, side, mark = together((near, side, mark))
        near_side = swap(near, 2)
        w_up, mark = load(mark, w_gate_up[0])
        far, mark = together((far, mark))
        last = swap(far, 4)
        mixed = jnp.stack((own, near, side, near_side))
        mixed, far = together((mixed, far))
        far_side = swap(far, 2)
        even, odd = terms(mixed, swap(mixed, 1))
        last, far_side, even = together((last, far_side, even))
        last_side = swap(last, 2)
        far_mixed = jnp.stack((far, far_side))
        far_even, far_odd = terms(far_mixed, swap(far_mixed, 1))
        last_side, far_even = together((last_side, far_even))
        last_mixed = jnp.stack((last, last_side))
        last_even, last_odd = terms(last_mixed, swap(last_mixed, 1))

        odd, far_odd, last_odd = swap(odd, 1), swap(far_odd, 1), swap(last_odd, 1)
        near_away = swap(add(even[3], odd[3]), 2)
        far_send, near_away = together((add(far_even[1], far_odd[1]), near_away))
        near_sum = add(even[1], odd[1], near_away)
        near_back = swap(near_sum, 4)
        far_sum = add(far_even[0], far_odd[0], swap(far_send, 2))
        last_away = swap(add(last_even[1], last_odd[1]), 2)
        own_send, last_away, near_back = together((add(even[2], odd[2]), last_away, near_back))
        last_sum = add(last_even[0], last_odd[0], last_away)
        return add(
            residual,
            even[0],
            odd[0],
            swap(own_send, 2),
            near_back,
            swap(far_sum, 8),
            swap(last_sum, 12),
        )
    w_up, mark = load(mark, w_gate_up[0])
    blocks = {0: own}
    mask = n // 2
    while mask > 1:
        for r in list(blocks):
            blocks[r ^ mask] = swap(blocks[r], mask)
        mask //= 2
    parts = {}
    for r in sorted(blocks):
        mixed = blocks[r][None]
        even, odd = terms(mixed, swap(mixed, 1))
        parts[r] = add(even, swap(odd, 1))[0]
    mask = 2
    while mask < n:
        parts = {r: add(parts[r], swap(parts[r ^ mask], mask)) for r in parts if not r & mask}
        mask *= 2
    return add(residual, parts[0])


def solution(mesh):
    placed = (
        P(("groups", "expert"), None),
        P(),
        P(("groups", "expert"), None),
        P(("groups", "expert"), None),
        P("expert", None, None),
        P("expert", None, None),
    )
    return jax.shard_map(
        local, mesh=mesh, in_specs=placed, out_specs=P(("groups", "expert"), None), check_vma=False
    )
```

time: 86.2 us -> 64.2 us (0.74)
  waiting for transfers between devices: 36.2 us -> 16.6 us
  Pallas kernels: 0 us -> 16.5 us
  matrix products: 11.8 us -> 0 us
  local copies, waits for them, and re-layouts: 11.4 us -> 0.01 us
  starting transfers between devices: 19 us -> 28.9 us
  other arithmetic: 7.29 us -> 1.47 us
    ppermute x30 -> x20, waiting for transfers between devices: 36.2 us -> 16.6 us  [swap(): return lax.ppermute(x, 'expert', [(i, i ^ mask) for i in range(n)])]
    pallas_call x0 -> x7, Pallas kernels: none -> 16.5 us  [the longest x3 9.56 us: mlp(): pl.pallas_call(functools.partial(mlp_kernel, experts, count), out_shape=[...]
    dot_general x2 -> x0, matrix products: 11.8 us -> none  [the longest x1 8.47 us: local(): jnp.dot(rows[:, :width], w_gate_up[0], preferred_element_type=jnp.float32)]
    unnamed x21 -> x2, local copies, waits for them, and re-layouts: 10.4 us -> 0.01 us
    ppermute x30 -> x20, starting transfers between devices: 19 us -> 28.9 us  [swap(): return lax.ppermute(x, 'expert', [(i, i ^ mask) for i in range(n)])]
    reduce_sum x4 -> x0, other arithmetic: 3.58 us -> none  [the longest x1 1.11 us: local(): jnp.sum(jnp.where(column == mine, tail, 0.0), axis=1, keepdims=True)]
    convert_element_type x2 -> x0, other arithmetic: 1.05 us -> none  [the longest x1 1.05 us: rms_scale(): return (values * lax.rsqrt(meansq + 1e-05) * gain).astype(jnp.bfloat16)]
  transfers between devices with their start and end apart: 30 -> 20, of which waited for: 12 -> 8; matrix products, arithmetic and copies ran while one was open for 13% -> 1% of each run, Pallas kernels for 0% -> 24%
where the time goes in v2:
time: 64.2 us; the launch traced here: 63.6 us
  starting transfers between devices  28.9 us (45%)
  waiting for transfers between devices  16.6 us (26%)
  Pallas kernels  16.5 us (26%)
  other arithmetic  1.47 us (2%)
    ppermute x20, starting transfers between devices, swap(): return lax.ppermute(x, 'expert', [(i, i ^ mask) for i in range(n)])  28.9 us
    ppermute x20, waiting for transfers between devices, swap(): return lax.ppermute(x, 'expert', [(i, i ^ mask) for i in range(n)])  16.6 us
    pallas_call x3, Pallas kernels, mlp(): pl.pallas_call(functools.partial(mlp_kernel, experts, count), out_shape=[...  9.56 us
    pallas_call x2, Pallas kernels, load(): pl.pallas_call(load_kernel, out_shape=[pltpu.VMEM(weight.shape, weight.dt...  5.78 us
  transfers between devices with their start and end apart: 20, of which 8 were waited for; matrix products, arithmetic and copies ran while one was open for 1% of the time, Pallas kernels for 24%

profile of v2, /device:TPU:0, one launch (start us, length us, event | category | flops | bytes accessed | tf_op | source)
XLA Modules:
  0.0 63.6 jit_solution(2039611238861568037)
XLA Ops:
  0.0 1.1 %pack.1.source.refs_1_ = bf16[32,2944]{1,0:T(8,128)(2,1)S(1)} custom-call(s32[1]{0:T(128)} %bitcast._.mine_ref, bf16[32,2880]{1,0:T(8,128)(2,1)} %residual_hbm.1, f32[2880]{0:T(1024)} %gain_hbm.1, s32[4,32]{1,0:T(4,128)} %bitcast.53, f32[4,32]{1,0:T(4,128)} %bitcast.54), custom_call_target="tpu_custom_call" | custom-call | tf_op jit(solution)/shard_map/pack/pallas_call | solution.py:61
  1.2 3.1 %collective-permute-start.1 = (bf16[32,2944]{1,0:T(8,128)(2,1)S(1)}, bf16[32,2944]{1,0:T(8,128)(2,1)S(1)}, u32[]{:S(2)}, u32[]{:S(2)}) collective-permute-start(bf16[32,2944]{1,0:T(8,128)(2,1)S(1)} %again.1), channel_id=1, source_target_pairs={{0,4},{1,5},{2,6},{3,7},{4,0},{5,1},{6,2},{7,3},{8,12},{9,13},{10,... | collective-permute-start | bytes 565256 | tf_op jit(solution)/shard_map/ppermute | solution.py:169
  4.3 1.5 %collective-permute-start.2 = (bf16[32,2944]{1,0:T(8,128)(2,1)S(1)}, bf16[32,2944]{1,0:T(8,128)(2,1)S(1)}, u32[]{:S(2)}, u32[]{:S(2)}) collective-permute-start(bf16[32,2944]{1,0:T(8,128)(2,1)S(1)} %again.1), channel_id=1, source_target_pairs={{0,2},{1,3},{2,0},{3,1},{4,6},{5,7},{6,4},{7,5},{8,10},{9,11},{10,... | collective-permute-start | bytes 565256 | tf_op jit(solution)/shard_map/ppermute | solution.py:169
  5.8 2.6 %collective-permute-start = (bf16[32,2944]{1,0:T(8,128)(2,1)S(1)}, bf16[32,2944]{1,0:T(8,128)(2,1)S(1)}, u32[]{:S(2)}, u32[]{:S(2)}) collective-permute-start(bf16[32,2944]{1,0:T(8,128)(2,1)S(1)} %pack.1.source.refs_1_), channel_id=1, source_target_pairs={{0,8},{1,9},{2,10},{3,11},{4,12},{5,13},{6,14},{7,15},{8,0},{9,1},... | collective-permute-start | bytes 565256 | tf_op jit(solution)/shard_map/ppermute | solution.py:169
  8.4 2.3 %load.2 = (bf16[2880,768]{1,0:T(8,128)(2,1)S(1)}, f32[8,128]{1,0:T(8,128)S(1)}) custom-call(bf16[2880,768]{1,0:T(8,128)(2,1)} %bitcast.45, bf16[32,2944]{1,0:T(8,128)(2,1)S(1)} %pack.1.source.refs_1_), custom_call_target="tpu_custom_call" | custom-call | bytes 4423680 | tf_op jit(solution)/shard_map/load/pallas_call | solution.py:102
  10.8 3.6 %collective-permute-start.4 = (bf16[32,2944]{1,0:T(8,128)(2,1)S(1)}, bf16[32,2944]{1,0:T(8,128)(2,1)S(1)}, u32[]{:S(2)}, u32[]{:S(2)}) collective-permute-start(bf16[32,2944]{1,0:T(8,128)(2,1)S(1)} %collective-permute-done.1), channel_id=1, source_target_pairs={{0,2},{1,3},{2,0},{3,1},{4,6},{5,7},{6,4},{7,5},{8,10},{9,11},{10,... | collective-permute-start | bytes 565256 | tf_op jit(solution)/shard_map/ppermute | solution.py:169
  14.4 3.5 %load.3 = (bf16[2880,1536]{1,0:T(8,128)(2,1)S(1)}, f32[8,128]{1,0:T(8,128)S(1)}) custom-call(bf16[2880,1536]{1,0:T(8,128)(2,1)} %bitcast.44, f32[8,128]{1,0:T(8,128)S(1)} %get-tuple-element.33.refs_1_), custom_call_target="tpu_custom_call" | custom-call | bytes 8847360 | tf_op jit(solution)/shard_map/load/pallas_call | solution.py:102
  18.2 2.1 %collective-permute-start.5 = (bf16[32,2944]{1,0:T(8,128)(2,1)S(1)}, bf16[32,2944]{1,0:T(8,128)(2,1)S(1)}, u32[]{:S(2)}, u32[]{:S(2)}) collective-permute-start(bf16[32,2944]{1,0:T(8,128)(2,1)S(1)} %collective-permute-done), channel_id=1, source_target_pairs={{0,2},{1,3},{2,0},{3,1},{4,6},{5,7},{6,4},{7,5},{8,10},{9,11},{10,... | collective-permute-start | bytes 565256 | tf_op jit(solution)/shard_map/ppermute | solution.py:169
  20.4 3.9 %mlp.3 = (bf16[4,32,2880]{2,1,0:T(8,128)(2,1)S(1)}, bf16[4,32,2880]{2,1,0:T(8,128)(2,1)S(1)}) custom-call(s32[1]{0:T(128)} %bitcast._.mine_ref, f32[8,128]{1,0:T(8,128)S(1)} %get-tuple-element.39.mark_ref, bf16[4,32,2944]{2,1,0:T(8,128)(2,1)S(1)} %pad_maximum_fusion.refs_0_, bf16[4,32,2944]{2,1,0:T(8,128)(2,1)S(1)} %collective-permute-done.6.refs_1_, ...), custom_call_target="tpu_custom_call" | custom-call | flops 3397386240 | bytes 13271040 | tf_op jit(solution)/shard_map/mlp/pallas_call | solution.py:150
  24.3 1.0 %collective-permute-done.3 = bf16[32,2944]{1,0:T(8,128)(2,1)S(1)} collective-permute-done((bf16[32,2944]{1,0:T(8,128)(2,1)S(1)}, bf16[32,2944]{1,0:T(8,128)(2,1)S(1)}, u32[]{:S(2)}, u32[]{:S(2)}) %collective-permute-start.3) | collective-permute-done | bytes 188448 | tf_op jit(solution)/shard_map/ppermute | solution.py:169
  26.2 1.8 %collective-permute-start.8 = (bf16[32,2944]{1,0:T(8,128)(2,1)S(1)}, bf16[32,2944]{1,0:T(8,128)(2,1)S(1)}, u32[]{:S(2)}, u32[]{:S(2)}) collective-permute-start(bf16[32,2944]{1,0:T(8,128)(2,1)S(1)} %collective-permute-done.3), channel_id=1, source_target_pairs={{0,2},{1,3},{2,0},{3,1},{4,6},{5,7},{6,4},{7,5},{8,10},{9,11},{10,... | collective-permute-start | bytes 565256 | tf_op jit(solution)/shard_map/ppermute | solution.py:169
  27.9 2.8 %mlp.4 = (bf16[2,32,2880]{2,1,0:T(8,128)(2,1)S(1)}, bf16[2,32,2880]{2,1,0:T(8,128)(2,1)S(1)}) custom-call(s32[1]{0:T(128)} %bitcast._.mine_ref, f32[8,128]{1,0:T(8,128)S(1)} %get-tuple-element.39.mark_ref, bf16[2,32,2944]{2,1,0:T(8,128)(2,1)S(1)} %pad_maximum_fusion.1.refs_0_, bf16[2,32,2944]{2,1,0:T(8,128)(2,1)S(1)} %collective-permute-done.9.refs_1_, ...), custom_call_target="tpu_custom_call" | custom-call | flops 1698693120 | bytes 13271040 | tf_op jit(solution)/shard_map/mlp/pallas_call | solution.py:150
  30.8 2.0 %collective-permute-done.8 = bf16[32,2944]{1,0:T(8,128)(2,1)S(1)} collective-permute-done((bf16[32,2944]{1,0:T(8,128)(2,1)S(1)}, bf16[32,2944]{1,0:T(8,128)(2,1)S(1)}, u32[]{:S(2)}, u32[]{:S(2)}) %collective-permute-start.8) | collective-permute-done | bytes 188448 | tf_op jit(solution)/shard_map/ppermute | solution.py:169
  33.1 1.8 %collective-permute-start.14 = (bf16[32,2880]{1,0:T(8,128)(2,1)S(1)}, bf16[32,2880]{1,0:T(8,128)(2,1)S(1)}, u32[]{:S(2)}, u32[]{:S(2)}) collective-permute-start(bf16[32,2880]{1,0:T(8,128)(2,1)S(1)} %get-tuple-element.59), channel_id=1, source_target_pairs={{0,2},{1,3},{2,0},{3,1},{4,6},{5,7},{6,4},{7,5},{8,10},{9,11},{10,... | collective-permute-start | bytes 552968 | tf_op jit(solution)/shard_map/ppermute | solution.py:169
  35.0 2.8 %mlp.5 = (bf16[2,32,2880]{2,1,0:T(8,128)(2,1)S(1)}, bf16[2,32,2880]{2,1,0:T(8,128)(2,1)S(1)}) custom-call(s32[1]{0:T(128)} %bitcast._.mine_ref, f32[8,128]{1,0:T(8,128)S(1)} %get-tuple-element.39.mark_ref, bf16[2,32,2944]{2,1,0:T(8,128)(2,1)S(1)} %pad_maximum_fusion.2.refs_0_, bf16[2,32,2944]{2,1,0:T(8,128)(2,1)S(1)} %collective-permute-done.10.refs_1_, ...), custom_call_target="tpu_custom_call" | custom-call | flops 1698693120 | bytes 13271040 | tf_op jit(solution)/shard_map/mlp/pallas_call | solution.py:150
  38.1 2.2 %collective-permute-done.14 = bf16[32,2880]{1,0:T(8,128)(2,1)S(1)} collective-permute-done((bf16[32,2880]{1,0:T(8,128)(2,1)S(1)}, bf16[32,2880]{1,0:T(8,128)(2,1)S(1)}, u32[]{:S(2)}, u32[]{:S(2)}) %collective-permute-start.14) | collective-permute-done | bytes 184352 | tf_op jit(solution)/shard_map/ppermute | solution.py:169
  40.3 1.7 %collective-permute-start.17 = (bf16[32,2880]{1,0:T(8,128)(2,1)S(1)}, bf16[32,2880]{1,0:T(8,128)(2,1)S(1)}, u32[]{:S(2)}, u32[]{:S(2)}) collective-permute-start(bf16[32,2880]{1,0:T(8,128)(2,1)S(1)} %fusion.10), channel_id=1, source_target_pairs={{0,2},{1,3},{2,0},{3,1},{4,6},{5,7},{6,4},{7,5},{8,10},{9,11},{10,... | collective-permute-start | bytes 552968 | tf_op jit(solution)/shard_map/ppermute | solution.py:169
  42.2 1.8 %collective-permute-start.15 = (bf16[32,2880]{1,0:T(8,128)(2,1)S(1)}, bf16[32,2880]{1,0:T(8,128)(2,1)S(1)}, u32[]{:S(2)}, u32[]{:S(2)}) collective-permute-start(bf16[32,2880]{1,0:T(8,128)(2,1)S(1)} %fusion.7), channel_id=1, source_target_pairs={{0,4},{1,5},{2,6},{3,7},{4,0},{5,1},{6,2},{7,3},{8,12},{9,13},{10,... | collective-permute-start | bytes 552968 | tf_op jit(solution)/shard_map/ppermute | solution.py:169
  44.4 3.1 %collective-permute-done.17 = bf16[32,2880]{1,0:T(8,128)(2,1)S(1)} collective-permute-done((bf16[32,2880]{1,0:T(8,128)(2,1)S(1)}, bf16[32,2880]{1,0:T(8,128)(2,1)S(1)}, u32[]{:S(2)}, u32[]{:S(2)}) %collective-permute-start.17) | collective-permute-done | bytes 184352 | tf_op jit(solution)/shard_map/ppermute | solution.py:169
  47.5 3.3 %collective-permute-start.18 = (bf16[32,2880]{1,0:T(8,128)(2,1)S(1)}, bf16[32,2880]{1,0:T(8,128)(2,1)S(1)}, u32[]{:S(2)}, u32[]{:S(2)}) collective-permute-start(bf16[32,2880]{1,0:T(8,128)(2,1)S(1)} %fusion.6), channel_id=1, source_target_pairs={{0,8},{1,9},{2,10},{3,11},{4,12},{5,13},{6,14},{7,15},{8,0},{9,1},... | collective-permute-start | bytes 552968 | tf_op jit(solution)/shard_map/ppermute | solution.py:169
  50.9 2.4 %collective-permute-start.19 = (bf16[32,2880]{1,0:T(8,128)(2,1)S(1)}, bf16[32,2880]{1,0:T(8,128)(2,1)S(1)}, u32[]{:S(2)}, u32[]{:S(2)}) collective-permute-start(bf16[32,2880]{1,0:T(8,128)(2,1)S(1)} %fusion.5), channel_id=1, source_target_pairs={{0,12},{1,13},{2,14},{3,15},{4,8},{5,9},{6,10},{7,11},{8,4},{9,5},... | collective-permute-start | bytes 552968 | tf_op jit(solution)/shard_map/ppermute | solution.py:169
  53.3 1.7 %collective-permute-start.16 = (bf16[32,2880]{1,0:T(8,128)(2,1)S(1)}, bf16[32,2880]{1,0:T(8,128)(2,1)S(1)}, u32[]{:S(2)}, u32[]{:S(2)}) collective-permute-start(bf16[32,2880]{1,0:T(8,128)(2,1)S(1)} %get-tuple-element.55), channel_id=1, source_target_pairs={{0,2},{1,3},{2,0},{3,1},{4,6},{5,7},{6,4},{7,5},{8,10},{9,11},{10,... | collective-permute-start | bytes 552968 | tf_op jit(solution)/shard_map/ppermute | solution.py:169
  55.1 7.7 %collective-permute-done.18 = bf16[32,2880]{1,0:T(8,128)(2,1)S(1)} collective-permute-done((bf16[32,2880]{1,0:T(8,128)(2,1)S(1)}, bf16[32,2880]{1,0:T(8,128)(2,1)S(1)}, u32[]{:S(2)}, u32[]{:S(2)}) %collective-permute-start.18) | collective-permute-done | bytes 184352 | tf_op jit(solution)/shard_map/ppermute | solution.py:169
  62.8 0.9 %fusion.4 = bf16[32,2880]{1,0:T(8,128)(2,1)} fusion(bf16[32,2880]{1,0:T(8,128)(2,1)S(1)} %collective-permute-done.19, bf16[32,2880]{1,0:T(8,128)(2,1)S(1)} %collective-permute-done.18, bf16[32,2880]{1,0:T(8,128)(2,1)S(1)} %collective-permute-done.15, bf16[32,2880]{1,0:T(8,128)(2,1)S(1)} %collective-permute-done.16, bf16[32,2880]{1,0:T(8,128)(2,1)S(1)} %copy-done, ...), kind=kLoop, calls=%fused_computation.8 | loop fusion | flops 1290240 | bytes 1474560 | tf_op jit(solution)/shard_map/convert_element_type | solution.py:176
  (35 shorter events, 2.7 us)
Async XLA Ops:
  1.2 9.6 %collective-permute-start.1 = (bf16[32,2944]{1,0:T(8,128)(2,1)S(1)}, bf16[32,2944]{1,0:T(8,128)(2,1)S(1)}, u32[]{:S(2)}, u32[]{:S(2)}) collective-permute-start(bf16[32,2944]{1,0:T(8,128)(2,1)S(1)} %again.1), channel_id=1, source_target_pairs={{0,4},{1,5},{2,6},{3,7},{4,0},{5,1},{6,2},{7,3},{8,12},{9,13},{10,... | collective-permute-start | bytes 565256 | tf_op jit(solution)/shard_map/ppermute | solution.py:169
  4.3 6.5 %collective-permute-start.2 = (bf16[32,2944]{1,0:T(8,128)(2,1)S(1)}, bf16[32,2944]{1,0:T(8,128)(2,1)S(1)}, u32[]{:S(2)}, u32[]{:S(2)}) collective-permute-start(bf16[32,2944]{1,0:T(8,128)(2,1)S(1)} %again.1), channel_id=1, source_target_pairs={{0,2},{1,3},{2,0},{3,1},{4,6},{5,7},{6,4},{7,5},{8,10},{9,11},{10,... | collective-permute-start | bytes 565256 | tf_op jit(solution)/shard_map/ppermute | solution.py:169
  5.8 12.1 %collective-permute-start = (bf16[32,2944]{1,0:T(8,128)(2,1)S(1)}, bf16[32,2944]{1,0:T(8,128)(2,1)S(1)}, u32[]{:S(2)}, u32[]{:S(2)}) collective-permute-start(bf16[32,2944]{1,0:T(8,128)(2,1)S(1)} %pack.1.source.refs_1_), channel_id=1, source_target_pairs={{0,8},{1,9},{2,10},{3,11},{4,12},{5,13},{6,14},{7,15},{8,0},{9,1},... | collective-permute-start | bytes 565256 | tf_op jit(solution)/shard_map/ppermute | solution.py:169
  10.8 7.1 %collective-permute-start.4 = (bf16[32,2944]{1,0:T(8,128)(2,1)S(1)}, bf16[32,2944]{1,0:T(8,128)(2,1)S(1)}, u32[]{:S(2)}, u32[]{:S(2)}) collective-permute-start(bf16[32,2944]{1,0:T(8,128)(2,1)S(1)} %collective-permute-done.1), channel_id=1, source_target_pairs={{0,2},{1,3},{2,0},{3,1},{4,6},{5,7},{6,4},{7,5},{8,10},{9,11},{10,... | collective-permute-start | bytes 565256 | tf_op jit(solution)/shard_map/ppermute | solution.py:169
  18.1 2.3 %collective-permute-start.6 = (bf16[4,32,2944]{2,1,0:T(8,128)(2,1)S(1)}, bf16[4,32,2944]{2,1,0:T(8,128)(2,1)S(1)}, u32[]{:S(2)}, u32[]{:S(2)}) collective-permute-start(bf16[4,32,2944]{2,1,0:T(8,128)(2,1)S(1)} %pad_maximum_fusion.refs_0_), channel_id=1, source_target_pairs={{0,1},{1,0},{2,3},{3,2},{4,5},{5,4},{6,7},{7,6},{8,9},{9,8},{10,11... | collective-permute-start | bytes 2261000 | tf_op jit(solution)/shard_map/ppermute | solution.py:169
  18.1 7.1 %collective-permute-start.3 = (bf16[32,2944]{1,0:T(8,128)(2,1)S(1)}, bf16[32,2944]{1,0:T(8,128)(2,1)S(1)}, u32[]{:S(2)}, u32[]{:S(2)}) collective-permute-start(bf16[32,2944]{1,0:T(8,128)(2,1)S(1)} %collective-permute-done), channel_id=1, source_target_pairs={{0,4},{1,5},{2,6},{3,7},{4,0},{5,1},{6,2},{7,3},{8,12},{9,13},{10,... | collective-permute-start | bytes 565256 | tf_op jit(solution)/shard_map/ppermute | solution.py:169
  18.2 7.3 %collective-permute-start.5 = (bf16[32,2944]{1,0:T(8,128)(2,1)S(1)}, bf16[32,2944]{1,0:T(8,128)(2,1)S(1)}, u32[]{:S(2)}, u32[]{:S(2)}) collective-permute-start(bf16[32,2944]{1,0:T(8,128)(2,1)S(1)} %collective-permute-done), channel_id=1, source_target_pairs={{0,2},{1,3},{2,0},{3,1},{4,6},{5,7},{6,4},{7,5},{8,10},{9,11},{10,... | collective-permute-start | bytes 565256 | tf_op jit(solution)/shard_map/ppermute | solution.py:169
  25.6 2.3 %collective-permute-start.9 = (bf16[2,32,2944]{2,1,0:T(8,128)(2,1)S(1)}, bf16[2,32,2944]{2,1,0:T(8,128)(2,1)S(1)}, u32[]{:S(2)}, u32[]{:S(2)}) collective-permute-start(bf16[2,32,2944]{2,1,0:T(8,128)(2,1)S(1)} %pad_maximum_fusion.1.refs_0_), channel_id=1, source_target_pairs={{0,1},{1,0},{2,3},{3,2},{4,5},{5,4},{6,7},{7,6},{8,9},{9,8},{10,11... | collective-permute-start | bytes 1130504 | tf_op jit(solution)/shard_map/ppermute | solution.py:169
  25.7 7.3 %collective-permute-start.7 = (bf16[4,32,2880]{2,1,0:T(8,128)(2,1)S(1)}, bf16[4,32,2880]{2,1,0:T(8,128)(2,1)S(1)}, u32[]{:S(2)}, u32[]{:S(2)}) collective-permute-start(bf16[4,32,2880]{2,1,0:T(8,128)(2,1)S(1)} %get-tuple-element.45), channel_id=1, source_target_pairs={{0,1},{1,0},{2,3},{3,2},{4,5},{5,4},{6,7},{7,6},{8,9},{9,8},{10,11... | collective-permute-start | bytes 2211848 | tf_op jit(solution)/shard_map/ppermute | solution.py:169
  26.2 6.7 %collective-permute-start.8 = (bf16[32,2944]{1,0:T(8,128)(2,1)S(1)}, bf16[32,2944]{1,0:T(8,128)(2,1)S(1)}, u32[]{:S(2)}, u32[]{:S(2)}) collective-permute-start(bf16[32,2944]{1,0:T(8,128)(2,1)S(1)} %collective-permute-done.3), channel_id=1, source_target_pairs={{0,2},{1,3},{2,0},{3,1},{4,6},{5,7},{6,4},{7,5},{8,10},{9,11},{10,... | collective-permute-start | bytes 565256 | tf_op jit(solution)/shard_map/ppermute | solution.py:169
  30.8 4.2 %collective-permute-start.13 = (bf16[2,32,2880]{2,1,0:T(8,128)(2,1)S(1)}, bf16[2,32,2880]{2,1,0:T(8,128)(2,1)S(1)}, u32[]{:S(2)}, u32[]{:S(2)}) collective-permute-start(bf16[2,32,2880]{2,1,0:T(8,128)(2,1)S(1)} %get-tuple-element.53), channel_id=1, source_target_pairs={{0,1},{1,0},{2,3},{3,2},{4,5},{5,4},{6,7},{7,6},{8,9},{9,8},{10,11... | collective-permute-start | bytes 1105928 | tf_op jit(solution)/shard_map/ppermute | solution.py:169
  32.9 2.1 %collective-permute-start.10 = (bf16[2,32,2944]{2,1,0:T(8,128)(2,1)S(1)}, bf16[2,32,2944]{2,1,0:T(8,128)(2,1)S(1)}, u32[]{:S(2)}, u32[]{:S(2)}) collective-permute-start(bf16[2,32,2944]{2,1,0:T(8,128)(2,1)S(1)} %pad_maximum_fusion.2.refs_0_), channel_id=1, source_target_pairs={{0,1},{1,0},{2,3},{3,2},{4,5},{5,4},{6,7},{7,6},{8,9},{9,8},{10,11... | collective-permute-start | bytes 1130504 | tf_op jit(solution)/shard_map/ppermute | solution.py:169
  33.1 29.6 %copy-start = (bf16[32,2880]{1,0:T(8,128)(2,1)S(1)}, bf16[32,2880]{1,0:T(8,128)(2,1)}, u32[]{:S(2)}) copy-start(bf16[32,2880]{1,0:T(8,128)(2,1)} %residual_hbm.1) | copy-start | bytes 552964
  33.1 7.2 %collective-permute-start.14 = (bf16[32,2880]{1,0:T(8,128)(2,1)S(1)}, bf16[32,2880]{1,0:T(8,128)(2,1)S(1)}, u32[]{:S(2)}, u32[]{:S(2)}) collective-permute-start(bf16[32,2880]{1,0:T(8,128)(2,1)S(1)} %get-tuple-element.59), channel_id=1, source_target_pairs={{0,2},{1,3},{2,0},{3,1},{4,6},{5,7},{6,4},{7,5},{8,10},{9,11},{10,... | collective-permute-start | bytes 552968 | tf_op jit(solution)/shard_map/ppermute | solution.py:169
  37.8 6.1 %collective-permute-start.11 = (bf16[2,32,2880]{2,1,0:T(8,128)(2,1)S(1)}, bf16[2,32,2880]{2,1,0:T(8,128)(2,1)S(1)}, u32[]{:S(2)}, u32[]{:S(2)}) collective-permute-start(bf16[2,32,2880]{2,1,0:T(8,128)(2,1)S(1)} %get-tuple-element.51), channel_id=1, source_target_pairs={{0,1},{1,0},{2,3},{3,2},{4,5},{5,4},{6,7},{7,6},{8,9},{9,8},{10,11... | collective-permute-start | bytes 1105928 | tf_op jit(solution)/shard_map/ppermute | solution.py:169
  40.3 7.1 %collective-permute-start.17 = (bf16[32,2880]{1,0:T(8,128)(2,1)S(1)}, bf16[32,2880]{1,0:T(8,128)(2,1)S(1)}, u32[]{:S(2)}, u32[]{:S(2)}) collective-permute-start(bf16[32,2880]{1,0:T(8,128)(2,1)S(1)} %fusion.10), channel_id=1, source_target_pairs={{0,2},{1,3},{2,0},{3,1},{4,6},{5,7},{6,4},{7,5},{8,10},{9,11},{10,... | collective-permute-start | bytes 552968 | tf_op jit(solution)/shard_map/ppermute | solution.py:169
  42.2 8.7 %collective-permute-start.15 = (bf16[32,2880]{1,0:T(8,128)(2,1)S(1)}, bf16[32,2880]{1,0:T(8,128)(2,1)S(1)}, u32[]{:S(2)}, u32[]{:S(2)}) collective-permute-start(bf16[32,2880]{1,0:T(8,128)(2,1)S(1)} %fusion.7), channel_id=1, source_target_pairs={{0,4},{1,5},{2,6},{3,7},{4,0},{5,1},{6,2},{7,3},{8,12},{9,13},{10,... | collective-permute-start | bytes 552968 | tf_op jit(solution)/shard_map/ppermute | solution.py:169
  44.0 6.8 %collective-permute-start.12 = (bf16[32,2880]{1,0:T(8,128)(2,1)S(1)}, bf16[32,2880]{1,0:T(8,128)(2,1)S(1)}, u32[]{:S(2)}, u32[]{:S(2)}) collective-permute-start(bf16[32,2880]{1,0:T(8,128)(2,1)S(1)} %fusion.9), channel_id=1, source_target_pairs={{0,2},{1,3},{2,0},{3,1},{4,6},{5,7},{6,4},{7,5},{8,10},{9,11},{10,... | collective-permute-start | bytes 552968 | tf_op jit(solution)/shard_map/ppermute | solution.py:169
  47.5 15.2 %collective-permute-start.18 = (bf16[32,2880]{1,0:T(8,128)(2,1)S(1)}, bf16[32,2880]{1,0:T(8,128)(2,1)S(1)}, u32[]{:S(2)}, u32[]{:S(2)}) collective-permute-start(bf16[32,2880]{1,0:T(8,128)(2,1)S(1)} %fusion.6), channel_id=1, source_target_pairs={{0,8},{1,9},{2,10},{3,11},{4,12},{5,13},{6,14},{7,15},{8,0},{9,1},... | collective-permute-start | bytes 552968 | tf_op jit(solution)/shard_map/ppermute | solution.py:169
  50.9 11.8 %collective-permute-start.19 = (bf16[32,2880]{1,0:T(8,128)(2,1)S(1)}, bf16[32,2880]{1,0:T(8,128)(2,1)S(1)}, u32[]{:S(2)}, u32[]{:S(2)}) collective-permute-start(bf16[32,2880]{1,0:T(8,128)(2,1)S(1)} %fusion.5), channel_id=1, source_target_pairs={{0,12},{1,13},{2,14},{3,15},{4,8},{5,9},{6,10},{7,11},{8,4},{9,5},... | collective-permute-start | bytes 552968 | tf_op jit(solution)/shard_map/ppermute | solution.py:169
  53.3 9.4 %collective-permute-start.16 = (bf16[32,2880]{1,0:T(8,128)(2,1)S(1)}, bf16[32,2880]{1,0:T(8,128)(2,1)S(1)}, u32[]{:S(2)}, u32[]{:S(2)}) collective-permute-start(bf16[32,2880]{1,0:T(8,128)(2,1)S(1)} %get-tuple-element.55), channel_id=1, source_target_pairs={{0,2},{1,3},{2,0},{3,1},{4,6},{5,7},{6,4},{7,5},{8,10},{9,11},{10,... | collective-permute-start | bytes 552968 | tf_op jit(solution)/shard_map/ppermute | solution.py:169

commit v3 on v2

--- a/solution.py
+++ b/solution.py
@@ -75,21 +75,6 @@
     )(mine, *in_hbm(residual, gain, ids.T, logits.T))
 
 
-def again_kernel(source, target):
-    target[...] = source[...]
-
-
-def again(x):
-    return pl.pallas_call(
-        again_kernel,
-        out_shape=jax.ShapeDtypeStruct(x.shape, x.dtype),
-        in_specs=[VMEM],
-        out_specs=VMEM,
-        compiler_params=pltpu.CompilerParams(vmem_limit_bytes=2 << 20),
-        name="again",
-    )(x)
-
-
 def load_kernel(*refs):
     source, _, target, mark, sem = refs
     copy = pltpu.make_async_copy(source, target, sem)
@@ -189,44 +174,40 @@
     if n == 16:
         together = lax.optimization_barrier
         far = swap(own, 8)
-        copied = again(own)
-        near = swap(copied, 4)
-        side = swap(copied, 2)
+        near = swap(own, 4)
+        side = swap(own, 2)
         near, side, mark = together((near, side, mark))
         near_side = swap(near, 2)
         w_up, mark = load(mark, w_gate_up[0])
         far, mark = together((far, mark))
         last = swap(far, 4)
-        mixed = jnp.stack((own, near, side, near_side))
+        mixed = jnp.stack((own, side, near, near_side))
         mixed, far = together((mixed, far))
         far_side = swap(far, 2)
         even, odd = terms(mixed, swap(mixed, 1))
         last, far_side, even = together((last, far_side, even))
         last_side = swap(last, 2)
         far_mixed = jnp.stack((far, far_side))
-        far_even, far_odd = terms(far_mixed, swap(far_mixed, 1))
+        far_other = swap(far_mixed, 1)
+        first = add(even, swap(odd, 1))
+        far_even, far_odd = terms(far_mixed, far_other)
         last_side, far_even = together((last_side, far_even))
         last_mixed = jnp.stack((last, last_side))
-        last_even, last_odd = terms(last_mixed, swap(last_mixed, 1))
-
-        odd, far_odd, last_odd = swap(odd, 1), swap(far_odd, 1), swap(last_odd, 1)
-        near_away = swap(add(even[3], odd[3]), 2)
-        far_send, near_away = together((add(far_even[1], far_odd[1]), near_away))
-        near_sum = add(even[1], odd[1], near_away)
-        near_back = swap(near_sum, 4)
-        far_sum = add(far_even[0], far_odd[0], swap(far_send, 2))
-        last_away = swap(add(last_even[1], last_odd[1]), 2)
-        own_send, last_away, near_back = together((add(even[2], odd[2]), last_away, near_back))
-        last_sum = add(last_even[0], last_odd[0], last_away)
-        return add(
-            residual,
-            even[0],
-            odd[0],
-            swap(own_send, 2),
-            near_back,
-            swap(far_sum, 8),
-            swap(last_sum, 12),
-        )
+        last_other = swap(last_mixed, 1)
+        far_sums = add(far_even, swap(far_odd, 1))
+        far_send = far_sums[1]
+        crossed = swap(first[2:], 4)
+        last_even, last_odd = terms(last_mixed, last_other)
+        last_sums = add(last_even, swap(last_odd, 1))
+        last_send = last_sums[1]
+        far_away = swap(far_send, 2)
+        last_away = swap(last_send, 2)
+        relayed = swap(add(far_sums[0], far_away), 4)
+        joined = add(last_sums[0], last_away, relayed)
+        own_send = add(first[1], crossed[1])
+        own_away = swap(own_send, 2)
+        last_back = swap(joined, 12)
+        return add(residual, first[0], crossed[0], own_away, last_back)
     w_up, mark = load(mark, w_gate_up[0])
     blocks = {0: own}
     mask = n // 2

time: 64.2 us -> 60 us (0.935)
  starting transfers between devices: 28.9 us -> 25.7 us
  waiting for transfers between devices: 16.6 us -> 15 us
    ppermute x20 -> x19, starting transfers between devices: 28.9 us -> 25.7 us  [swap(): return lax.ppermute(x, 'expert', [(i, i ^ mask) for i in range(n)])]
    ppermute x20 -> x19, waiting for transfers between devices: 16.6 us -> 15 us  [swap(): return lax.ppermute(x, 'expert', [(i, i ^ mask) for i in range(n)])]
  transfers between devices with their start and end apart: 20 -> 19, of which waited for: 8 -> 9; matrix products, arithmetic and copies ran while one was open for 1% -> 1% of each run, Pallas kernels for 24% -> 26%
where the time goes in v3:
time: 60 us; the launch traced here: 58.9 us
  starting transfers between devices  25.7 us (43%)
  Pallas kernels  16.5 us (28%)
  waiting for transfers between devices  15 us (25%)
  other arithmetic  1.51 us (3%)
    ppermute x19, starting transfers between devices, swap(): return lax.ppermute(x, 'expert', [(i, i ^ mask) for i in range(n)])  25.7 us
    ppermute x19, waiting for transfers between devices, swap(): return lax.ppermute(x, 'expert', [(i, i ^ mask) for i in range(n)])  15 us
    pallas_call x3, Pallas kernels, mlp(): pl.pallas_call(functools.partial(mlp_kernel, experts, count), out_shape=[...  9.56 us
    pallas_call x2, Pallas kernels, load(): pl.pallas_call(load_kernel, out_shape=[pltpu.VMEM(weight.shape, weight.dt...  5.78 us
    convert_element_type x7, other arithmetic, add(): return total.astype(jnp.bfloat16)  1.32 us
  transfers between devices with their start and end apart: 19, of which 9 were waited for; matrix products, arithmetic and copies ran while one was open for 1% of the time, Pallas kernels for 26%

profile of v3, /device:TPU:0, one launch (start us, length us, event | category | flops | bytes accessed | tf_op | source)
XLA Modules:
  0.0 58.9 jit_solution(8671315691716339037)
XLA Ops:
  0.0 1.1 %pack.1.refs_1_ = bf16[32,2944]{1,0:T(8,128)(2,1)S(1)} custom-call(s32[1]{0:T(128)} %bitcast._.mine_ref, bf16[32,2880]{1,0:T(8,128)(2,1)} %residual_hbm.1, f32[2880]{0:T(1024)} %gain_hbm.1, s32[4,32]{1,0:T(4,128)} %bitcast.51, f32[4,32]{1,0:T(4,128)} %bitcast.52), custom_call_target="tpu_custom_call" | custom-call | tf_op jit(solution)/shard_map/pack/pallas_call | solution.py:61
  1.2 3.1 %collective-permute-start.1 = (bf16[32,2944]{1,0:T(8,128)(2,1)S(1)}, bf16[32,2944]{1,0:T(8,128)(2,1)S(1)}, u32[]{:S(2)}, u32[]{:S(2)}) collective-permute-start(bf16[32,2944]{1,0:T(8,128)(2,1)S(1)} %pack.1.refs_1_), channel_id=1, source_target_pairs={{0,4},{1,5},{2,6},{3,7},{4,0},{5,1},{6,2},{7,3},{8,12},{9,13},{10,... | collective-permute-start | bytes 565256 | tf_op jit(solution)/shard_map/ppermute | solution.py:154
  4.2 1.5 %collective-permute-start.2 = (bf16[32,2944]{1,0:T(8,128)(2,1)S(1)}, bf16[32,2944]{1,0:T(8,128)(2,1)S(1)}, u32[]{:S(2)}, u32[]{:S(2)}) collective-permute-start(bf16[32,2944]{1,0:T(8,128)(2,1)S(1)} %pack.1.refs_1_), channel_id=1, source_target_pairs={{0,2},{1,3},{2,0},{3,1},{4,6},{5,7},{6,4},{7,5},{8,10},{9,11},{10,... | collective-permute-start | bytes 565256 | tf_op jit(solution)/shard_map/ppermute | solution.py:154
  5.8 2.6 %collective-permute-start = (bf16[32,2944]{1,0:T(8,128)(2,1)S(1)}, bf16[32,2944]{1,0:T(8,128)(2,1)S(1)}, u32[]{:S(2)}, u32[]{:S(2)}) collective-permute-start(bf16[32,2944]{1,0:T(8,128)(2,1)S(1)} %pack.1.refs_1_), channel_id=1, source_target_pairs={{0,8},{1,9},{2,10},{3,11},{4,12},{5,13},{6,14},{7,15},{8,0},{9,1},... | collective-permute-start | bytes 565256 | tf_op jit(solution)/shard_map/ppermute | solution.py:154
  8.4 2.3 %load.2 = (bf16[2880,768]{1,0:T(8,128)(2,1)S(1)}, f32[8,128]{1,0:T(8,128)S(1)}) custom-call(bf16[2880,768]{1,0:T(8,128)(2,1)} %bitcast.43, bf16[32,2944]{1,0:T(8,128)(2,1)S(1)} %pack.1.refs_1_), custom_call_target="tpu_custom_call" | custom-call | bytes 4423680 | tf_op jit(solution)/shard_map/load/pallas_call | solution.py:87
  10.8 3.6 %collective-permute-start.4 = (bf16[32,2944]{1,0:T(8,128)(2,1)S(1)}, bf16[32,2944]{1,0:T(8,128)(2,1)S(1)}, u32[]{:S(2)}, u32[]{:S(2)}) collective-permute-start(bf16[32,2944]{1,0:T(8,128)(2,1)S(1)} %collective-permute-done.1), channel_id=1, source_target_pairs={{0,2},{1,3},{2,0},{3,1},{4,6},{5,7},{6,4},{7,5},{8,10},{9,11},{10,... | collective-permute-start | bytes 565256 | tf_op jit(solution)/shard_map/ppermute | solution.py:154
  14.4 3.5 %load.3 = (bf16[2880,1536]{1,0:T(8,128)(2,1)S(1)}, f32[8,128]{1,0:T(8,128)S(1)}) custom-call(bf16[2880,1536]{1,0:T(8,128)(2,1)} %bitcast.42, f32[8,128]{1,0:T(8,128)S(1)} %get-tuple-element.28.refs_1_), custom_call_target="tpu_custom_call" | custom-call | bytes 8847360 | tf_op jit(solution)/shard_map/load/pallas_call | solution.py:87
  18.2 2.1 %collective-permute-start.5 = (bf16[32,2944]{1,0:T(8,128)(2,1)S(1)}, bf16[32,2944]{1,0:T(8,128)(2,1)S(1)}, u32[]{:S(2)}, u32[]{:S(2)}) collective-permute-start(bf16[32,2944]{1,0:T(8,128)(2,1)S(1)} %collective-permute-done), channel_id=1, source_target_pairs={{0,2},{1,3},{2,0},{3,1},{4,6},{5,7},{6,4},{7,5},{8,10},{9,11},{10,... | collective-permute-start | bytes 565256 | tf_op jit(solution)/shard_map/ppermute | solution.py:154
  20.3 3.9 %mlp.3 = (bf16[4,32,2880]{2,1,0:T(8,128)(2,1)S(1)}, bf16[4,32,2880]{2,1,0:T(8,128)(2,1)S(1)}) custom-call(s32[1]{0:T(128)} %bitcast._.mine_ref, f32[8,128]{1,0:T(8,128)S(1)} %get-tuple-element.34.mark_ref, bf16[4,32,2944]{2,1,0:T(8,128)(2,1)S(1)} %pad_maximum_fusion.refs_0_, bf16[4,32,2944]{2,1,0:T(8,128)(2,1)S(1)} %collective-permute-done.6.refs_1_, ...), custom_call_target="tpu_custom_call" | custom-call | flops 3397386240 | bytes 13271040 | tf_op jit(solution)/shard_map/mlp/pallas_call | solution.py:135
  24.2 1.0 %collective-permute-done.3 = bf16[32,2944]{1,0:T(8,128)(2,1)S(1)} collective-permute-done((bf16[32,2944]{1,0:T(8,128)(2,1)S(1)}, bf16[32,2944]{1,0:T(8,128)(2,1)S(1)}, u32[]{:S(2)}, u32[]{:S(2)}) %collective-permute-start.3) | collective-permute-done | bytes 188448 | tf_op jit(solution)/shard_map/ppermute | solution.py:154
  25.6 1.8 %collective-permute-start.10 = (bf16[32,2944]{1,0:T(8,128)(2,1)S(1)}, bf16[32,2944]{1,0:T(8,128)(2,1)S(1)}, u32[]{:S(2)}, u32[]{:S(2)}) collective-permute-start(bf16[32,2944]{1,0:T(8,128)(2,1)S(1)} %collective-permute-done.3), channel_id=1, source_target_pairs={{0,2},{1,3},{2,0},{3,1},{4,6},{5,7},{6,4},{7,5},{8,10},{9,11},{10,... | collective-permute-start | bytes 565256 | tf_op jit(solution)/shard_map/ppermute | solution.py:154
  27.5 2.8 %mlp.4 = (bf16[2,32,2880]{2,1,0:T(8,128)(2,1)S(1)}, bf16[2,32,2880]{2,1,0:T(8,128)(2,1)S(1)}) custom-call(s32[1]{0:T(128)} %bitcast._.mine_ref, f32[8,128]{1,0:T(8,128)S(1)} %get-tuple-element.34.mark_ref, bf16[2,32,2944]{2,1,0:T(8,128)(2,1)S(1)} %pad_maximum_fusion.1.refs_0_, bf16[2,32,2944]{2,1,0:T(8,128)(2,1)S(1)} %collective-permute-done.11.refs_1_, ...), custom_call_target="tpu_custom_call" | custom-call | flops 1698693120 | bytes 13271040 | tf_op jit(solution)/shard_map/mlp/pallas_call | solution.py:135
  30.9 1.9 %collective-permute-done.10 = bf16[32,2944]{1,0:T(8,128)(2,1)S(1)} collective-permute-done((bf16[32,2944]{1,0:T(8,128)(2,1)S(1)}, bf16[32,2944]{1,0:T(8,128)(2,1)S(1)}, u32[]{:S(2)}, u32[]{:S(2)}) %collective-permute-start.10) | collective-permute-done | bytes 188448 | tf_op jit(solution)/shard_map/ppermute | solution.py:154
  33.0 1.8 %collective-permute-start.16 = (bf16[32,2880]{1,0:T(8,128)(2,1)S(1)}, bf16[32,2880]{1,0:T(8,128)(2,1)S(1)}, u32[]{:S(2)}, u32[]{:S(2)}) collective-permute-start(bf16[32,2880]{1,0:T(8,128)(2,1)S(1)} %slice_bitcast_fusion), channel_id=1, source_target_pairs={{0,2},{1,3},{2,0},{3,1},{4,6},{5,7},{6,4},{7,5},{8,10},{9,11},{10,... | collective-permute-start | bytes 552968 | tf_op jit(solution)/shard_map/ppermute | solution.py:154
  35.1 1.8 %collective-permute-start.8 = (bf16[2,32,2880]{2,1,0:T(8,128)(2,1)S(1)}, bf16[2,32,2880]{2,1,0:T(8,128)(2,1)S(1)}, u32[]{:S(2)}, u32[]{:S(2)}) collective-permute-start(bf16[2,32,2880]{2,1,0:T(8,128)(2,1)S(1)} %slice.37), channel_id=1, source_target_pairs={{0,4},{1,5},{2,6},{3,7},{4,0},{5,1},{6,2},{7,3},{8,12},{9,13},{10,... | collective-permute-start | bytes 1105928 | tf_op jit(solution)/shard_map/ppermute | solution.py:154
  36.9 2.8 %mlp.5 = (bf16[2,32,2880]{2,1,0:T(8,128)(2,1)S(1)}, bf16[2,32,2880]{2,1,0:T(8,128)(2,1)S(1)}) custom-call(s32[1]{0:T(128)} %bitcast._.mine_ref, f32[8,128]{1,0:T(8,128)S(1)} %get-tuple-element.34.mark_ref, bf16[2,32,2944]{2,1,0:T(8,128)(2,1)S(1)} %pad_maximum_fusion.2.refs_0_, bf16[2,32,2944]{2,1,0:T(8,128)(2,1)S(1)} %collective-permute-done.12.refs_1_, ...), custom_call_target="tpu_custom_call" | custom-call | flops 1698693120 | bytes 13271040 | tf_op jit(solution)/shard_map/mlp/pallas_call | solution.py:135
  39.8 0.4 collective-permute-done.16
  40.3 1.8 %collective-permute-start.17 = (bf16[32,2880]{1,0:T(8,128)(2,1)S(1)}, bf16[32,2880]{1,0:T(8,128)(2,1)S(1)}, u32[]{:S(2)}, u32[]{:S(2)}) collective-permute-start(bf16[32,2880]{1,0:T(8,128)(2,1)S(1)} %fusion), channel_id=1, source_target_pairs={{0,4},{1,5},{2,6},{3,7},{4,0},{5,1},{6,2},{7,3},{8,12},{9,13},{10,... | collective-permute-start | bytes 552968 | tf_op jit(solution)/shard_map/ppermute | solution.py:154
  42.2 1.8 %collective-permute-start.14 = (bf16[32,2880]{1,0:T(8,128)(2,1)S(1)}, bf16[32,2880]{1,0:T(8,128)(2,1)S(1)}, u32[]{:S(2)}, u32[]{:S(2)}) collective-permute-start(bf16[32,2880]{1,0:T(8,128)(2,1)S(1)} %slice_bitcast_fusion.2), channel_id=1, source_target_pairs={{0,2},{1,3},{2,0},{3,1},{4,6},{5,7},{6,4},{7,5},{8,10},{9,11},{10,... | collective-permute-start | bytes 552968 | tf_op jit(solution)/shard_map/ppermute | solution.py:154
  44.0 2.7 %collective-permute-done.8 = bf16[2,32,2880]{2,1,0:T(8,128)(2,1)S(1)} collective-permute-done((bf16[2,32,2880]{2,1,0:T(8,128)(2,1)S(1)}, bf16[2,32,2880]{2,1,0:T(8,128)(2,1)S(1)}, u32[]{:S(2)}, u32[]{:S(2)}) %collective-permute-start.8) | collective-permute-done | bytes 368672 | tf_op jit(solution)/shard_map/ppermute | solution.py:154
  47.1 2.9 %collective-permute-done.17 = bf16[32,2880]{1,0:T(8,128)(2,1)S(1)} collective-permute-done((bf16[32,2880]{1,0:T(8,128)(2,1)S(1)}, bf16[32,2880]{1,0:T(8,128)(2,1)S(1)}, u32[]{:S(2)}, u32[]{:S(2)}) %collective-permute-start.17) | collective-permute-done | bytes 184352 | tf_op jit(solution)/shard_map/ppermute | solution.py:154
  50.2 2.5 %collective-permute-start.18 = (bf16[32,2880]{1,0:T(8,128)(2,1)S(1)}, bf16[32,2880]{1,0:T(8,128)(2,1)S(1)}, u32[]{:S(2)}, u32[]{:S(2)}) collective-permute-start(bf16[32,2880]{1,0:T(8,128)(2,1)S(1)} %fusion.2), channel_id=1, source_target_pairs={{0,12},{1,13},{2,14},{3,15},{4,8},{5,9},{6,10},{7,11},{8,4},{9,5},... | collective-permute-start | bytes 552968 | tf_op jit(solution)/shard_map/ppermute | solution.py:154
  52.7 5.4 %collective-permute-done.18 = bf16[32,2880]{1,0:T(8,128)(2,1)S(1)} collective-permute-done((bf16[32,2880]{1,0:T(8,128)(2,1)S(1)}, bf16[32,2880]{1,0:T(8,128)(2,1)S(1)}, u32[]{:S(2)}, u32[]{:S(2)}) %collective-permute-start.18) | collective-permute-done | bytes 184352 | tf_op jit(solution)/shard_map/ppermute | solution.py:154
  58.1 0.8 %fusion.5 = bf16[32,2880]{1,0:T(8,128)(2,1)} fusion(bf16[32,2880]{1,0:T(8,128)(2,1)S(1)} %collective-permute-done.18, bf16[32,2880]{1,0:T(8,128)(2,1)S(1)} %collective-permute-done.9, bf16[32,2880]{1,0:T(8,128)(2,1)S(1)} %copy-done, bf16[2,32,2880]{2,1,0:T(8,128)(2,1)S(1)} %collective-permute-done.8, bf16[4,32,2880]{2,1,0:T(8,128)(2,1)S(1)} %add_convert_fusion), kind=kLoop, calls=%fused_computation.14 | loop fusion | flops 921600 | bytes 1105920 | tf_op jit(solution)/shard_map/convert_element_type | solution.py:161
  (35 shorter events, 2.6 us)
Async XLA Ops:
  1.2 9.6 %collective-permute-start.1 = (bf16[32,2944]{1,0:T(8,128)(2,1)S(1)}, bf16[32,2944]{1,0:T(8,128)(2,1)S(1)}, u32[]{:S(2)}, u32[]{:S(2)}) collective-permute-start(bf16[32,2944]{1,0:T(8,128)(2,1)S(1)} %pack.1.refs_1_), channel_id=1, source_target_pairs={{0,4},{1,5},{2,6},{3,7},{4,0},{5,1},{6,2},{7,3},{8,12},{9,13},{10,... | collective-permute-start | bytes 565256 | tf_op jit(solution)/shard_map/ppermute | solution.py:154
  4.2 6.5 %collective-permute-start.2 = (bf16[32,2944]{1,0:T(8,128)(2,1)S(1)}, bf16[32,2944]{1,0:T(8,128)(2,1)S(1)}, u32[]{:S(2)}, u32[]{:S(2)}) collective-permute-start(bf16[32,2944]{1,0:T(8,128)(2,1)S(1)} %pack.1.refs_1_), channel_id=1, source_target_pairs={{0,2},{1,3},{2,0},{3,1},{4,6},{5,7},{6,4},{7,5},{8,10},{9,11},{10,... | collective-permute-start | bytes 565256 | tf_op jit(solution)/shard_map/ppermute | solution.py:154
  5.8 12.1 %collective-permute-start = (bf16[32,2944]{1,0:T(8,128)(2,1)S(1)}, bf16[32,2944]{1,0:T(8,128)(2,1)S(1)}, u32[]{:S(2)}, u32[]{:S(2)}) collective-permute-start(bf16[32,2944]{1,0:T(8,128)(2,1)S(1)} %pack.1.refs_1_), channel_id=1, source_target_pairs={{0,8},{1,9},{2,10},{3,11},{4,12},{5,13},{6,14},{7,15},{8,0},{9,1},... | collective-permute-start | bytes 565256 | tf_op jit(solution)/shard_map/ppermute | solution.py:154
  10.8 7.1 %collective-permute-start.4 = (bf16[32,2944]{1,0:T(8,128)(2,1)S(1)}, bf16[32,2944]{1,0:T(8,128)(2,1)S(1)}, u32[]{:S(2)}, u32[]{:S(2)}) collective-permute-start(bf16[32,2944]{1,0:T(8,128)(2,1)S(1)} %collective-permute-done.1), channel_id=1, source_target_pairs={{0,2},{1,3},{2,0},{3,1},{4,6},{5,7},{6,4},{7,5},{8,10},{9,11},{10,... | collective-permute-start | bytes 565256 | tf_op jit(solution)/shard_map/ppermute | solution.py:154
  18.0 2.3 %collective-permute-start.6 = (bf16[4,32,2944]{2,1,0:T(8,128)(2,1)S(1)}, bf16[4,32,2944]{2,1,0:T(8,128)(2,1)S(1)}, u32[]{:S(2)}, u32[]{:S(2)}) collective-permute-start(bf16[4,32,2944]{2,1,0:T(8,128)(2,1)S(1)} %pad_maximum_fusion.refs_0_), channel_id=1, source_target_pairs={{0,1},{1,0},{2,3},{3,2},{4,5},{5,4},{6,7},{7,6},{8,9},{9,8},{10,11... | collective-permute-start | bytes 2261000 | tf_op jit(solution)/shard_map/ppermute | solution.py:154
  18.1 7.1 %collective-permute-start.3 = (bf16[32,2944]{1,0:T(8,128)(2,1)S(1)}, bf16[32,2944]{1,0:T(8,128)(2,1)S(1)}, u32[]{:S(2)}, u32[]{:S(2)}) collective-permute-start(bf16[32,2944]{1,0:T(8,128)(2,1)S(1)} %collective-permute-done), channel_id=1, source_target_pairs={{0,4},{1,5},{2,6},{3,7},{4,0},{5,1},{6,2},{7,3},{8,12},{9,13},{10,... | collective-permute-start | bytes 565256 | tf_op jit(solution)/shard_map/ppermute | solution.py:154
  18.2 7.3 %collective-permute-start.5 = (bf16[32,2944]{1,0:T(8,128)(2,1)S(1)}, bf16[32,2944]{1,0:T(8,128)(2,1)S(1)}, u32[]{:S(2)}, u32[]{:S(2)}) collective-permute-start(bf16[32,2944]{1,0:T(8,128)(2,1)S(1)} %collective-permute-done), channel_id=1, source_target_pairs={{0,2},{1,3},{2,0},{3,1},{4,6},{5,7},{6,4},{7,5},{8,10},{9,11},{10,... | collective-permute-start | bytes 565256 | tf_op jit(solution)/shard_map/ppermute | solution.py:154
  25.6 1.9 %collective-permute-start.11 = (bf16[2,32,2944]{2,1,0:T(8,128)(2,1)S(1)}, bf16[2,32,2944]{2,1,0:T(8,128)(2,1)S(1)}, u32[]{:S(2)}, u32[]{:S(2)}) collective-permute-start(bf16[2,32,2944]{2,1,0:T(8,128)(2,1)S(1)} %pad_maximum_fusion.1.refs_0_), channel_id=1, source_target_pairs={{0,1},{1,0},{2,3},{3,2},{4,5},{5,4},{6,7},{7,6},{8,9},{9,8},{10,11... | collective-permute-start | bytes 1130504 | tf_op jit(solution)/shard_map/ppermute | solution.py:154
  25.6 7.1 %collective-permute-start.10 = (bf16[32,2944]{1,0:T(8,128)(2,1)S(1)}, bf16[32,2944]{1,0:T(8,128)(2,1)S(1)}, u32[]{:S(2)}, u32[]{:S(2)}) collective-permute-start(bf16[32,2944]{1,0:T(8,128)(2,1)S(1)} %collective-permute-done.3), channel_id=1, source_target_pairs={{0,2},{1,3},{2,0},{3,1},{4,6},{5,7},{6,4},{7,5},{8,10},{9,11},{10,... | collective-permute-start | bytes 565256 | tf_op jit(solution)/shard_map/ppermute | solution.py:154
  30.3 2.6 %collective-permute-start.15 = (bf16[2,32,2880]{2,1,0:T(8,128)(2,1)S(1)}, bf16[2,32,2880]{2,1,0:T(8,128)(2,1)S(1)}, u32[]{:S(2)}, u32[]{:S(2)}) collective-permute-start(bf16[2,32,2880]{2,1,0:T(8,128)(2,1)S(1)} %get-tuple-element.48), channel_id=1, source_target_pairs={{0,1},{1,0},{2,3},{3,2},{4,5},{5,4},{6,7},{7,6},{8,9},{9,8},{10,11... | collective-permute-start | bytes 1105928 | tf_op jit(solution)/shard_map/ppermute | solution.py:154
  30.5 4.3 %collective-permute-start.7 = (bf16[4,32,2880]{2,1,0:T(8,128)(2,1)S(1)}, bf16[4,32,2880]{2,1,0:T(8,128)(2,1)S(1)}, u32[]{:S(2)}, u32[]{:S(2)}) collective-permute-start(bf16[4,32,2880]{2,1,0:T(8,128)(2,1)S(1)} %get-tuple-element.40), channel_id=1, source_target_pairs={{0,1},{1,0},{2,3},{3,2},{4,5},{5,4},{6,7},{7,6},{8,9},{9,8},{10,11... | collective-permute-start | bytes 2211848 | tf_op jit(solution)/shard_map/ppermute | solution.py:154
  32.8 4.1 %collective-permute-start.12 = (bf16[2,32,2944]{2,1,0:T(8,128)(2,1)S(1)}, bf16[2,32,2944]{2,1,0:T(8,128)(2,1)S(1)}, u32[]{:S(2)}, u32[]{:S(2)}) collective-permute-start(bf16[2,32,2944]{2,1,0:T(8,128)(2,1)S(1)} %pad_maximum_fusion.2.refs_0_), channel_id=1, source_target_pairs={{0,1},{1,0},{2,3},{3,2},{4,5},{5,4},{6,7},{7,6},{8,9},{9,8},{10,11... | collective-permute-start | bytes 1130504 | tf_op jit(solution)/shard_map/ppermute | solution.py:154
  33.0 7.2 %collective-permute-start.16 = (bf16[32,2880]{1,0:T(8,128)(2,1)S(1)}, bf16[32,2880]{1,0:T(8,128)(2,1)S(1)}, u32[]{:S(2)}, u32[]{:S(2)}) collective-permute-start(bf16[32,2880]{1,0:T(8,128)(2,1)S(1)} %slice_bitcast_fusion), channel_id=1, source_target_pairs={{0,2},{1,3},{2,0},{3,1},{4,6},{5,7},{6,4},{7,5},{8,10},{9,11},{10,... | collective-permute-start | bytes 552968 | tf_op jit(solution)/shard_map/ppermute | solution.py:154
  35.1 23.1 %copy-start = (bf16[32,2880]{1,0:T(8,128)(2,1)S(1)}, bf16[32,2880]{1,0:T(8,128)(2,1)}, u32[]{:S(2)}) copy-start(bf16[32,2880]{1,0:T(8,128)(2,1)} %residual_hbm.1) | copy-start | bytes 552964
  35.1 11.7 %collective-permute-start.8 = (bf16[2,32,2880]{2,1,0:T(8,128)(2,1)S(1)}, bf16[2,32,2880]{2,1,0:T(8,128)(2,1)S(1)}, u32[]{:S(2)}, u32[]{:S(2)}) collective-permute-start(bf16[2,32,2880]{2,1,0:T(8,128)(2,1)S(1)} %slice.37), channel_id=1, source_target_pairs={{0,4},{1,5},{2,6},{3,7},{4,0},{5,1},{6,2},{7,3},{8,12},{9,13},{10,... | collective-permute-start | bytes 1105928 | tf_op jit(solution)/shard_map/ppermute | solution.py:154
  39.7 2.4 %collective-permute-start.13 = (bf16[2,32,2880]{2,1,0:T(8,128)(2,1)S(1)}, bf16[2,32,2880]{2,1,0:T(8,128)(2,1)S(1)}, u32[]{:S(2)}, u32[]{:S(2)}) collective-permute-start(bf16[2,32,2880]{2,1,0:T(8,128)(2,1)S(1)} %get-tuple-element.46), channel_id=1, source_target_pairs={{0,1},{1,0},{2,3},{3,2},{4,5},{5,4},{6,7},{7,6},{8,9},{9,8},{10,11... | collective-permute-start | bytes 1105928 | tf_op jit(solution)/shard_map/ppermute | solution.py:154
  40.3 9.8 %collective-permute-start.17 = (bf16[32,2880]{1,0:T(8,128)(2,1)S(1)}, bf16[32,2880]{1,0:T(8,128)(2,1)S(1)}, u32[]{:S(2)}, u32[]{:S(2)}) collective-permute-start(bf16[32,2880]{1,0:T(8,128)(2,1)S(1)} %fusion), channel_id=1, source_target_pairs={{0,4},{1,5},{2,6},{3,7},{4,0},{5,1},{6,2},{7,3},{8,12},{9,13},{10,... | collective-permute-start | bytes 552968 | tf_op jit(solution)/shard_map/ppermute | solution.py:154
  42.2 7.9 %collective-permute-start.14 = (bf16[32,2880]{1,0:T(8,128)(2,1)S(1)}, bf16[32,2880]{1,0:T(8,128)(2,1)S(1)}, u32[]{:S(2)}, u32[]{:S(2)}) collective-permute-start(bf16[32,2880]{1,0:T(8,128)(2,1)S(1)} %slice_bitcast_fusion.2), channel_id=1, source_target_pairs={{0,2},{1,3},{2,0},{3,1},{4,6},{5,7},{6,4},{7,5},{8,10},{9,11},{10,... | collective-permute-start | bytes 552968 | tf_op jit(solution)/shard_map/ppermute | solution.py:154
  46.8 5.9 %collective-permute-start.9 = (bf16[32,2880]{1,0:T(8,128)(2,1)S(1)}, bf16[32,2880]{1,0:T(8,128)(2,1)S(1)}, u32[]{:S(2)}, u32[]{:S(2)}) collective-permute-start(bf16[32,2880]{1,0:T(8,128)(2,1)S(1)} %fusion.6), channel_id=1, source_target_pairs={{0,2},{1,3},{2,0},{3,1},{4,6},{5,7},{6,4},{7,5},{8,10},{9,11},{10,... | collective-permute-start | bytes 552968 | tf_op jit(solution)/shard_map/ppermute | solution.py:154
  50.2 8.0 %collective-permute-start.18 = (bf16[32,2880]{1,0:T(8,128)(2,1)S(1)}, bf16[32,2880]{1,0:T(8,128)(2,1)S(1)}, u32[]{:S(2)}, u32[]{:S(2)}) collective-permute-start(bf16[32,2880]{1,0:T(8,128)(2,1)S(1)} %fusion.2), channel_id=1, source_target_pairs={{0,12},{1,13},{2,14},{3,15},{4,8},{5,9},{6,10},{7,11},{8,4},{9,5},... | collective-permute-start | bytes 552968 | tf_op jit(solution)/shard_map/ppermute | solution.py:154

commit v4 on v3

--- a/solution.py
+++ b/solution.py
@@ -101,12 +101,13 @@
     )(*in_hbm(weight), after)
 
 
-def mlp_kernel(experts, count, mine_ref, mark_ref, *refs):
+def mlp_kernel(experts, counts, mine_ref, mark_ref, *refs):
+    count = len(counts)
     blocks, (w_up, w_dn) = refs[:count], refs[count : count + 2]
     even_ref, odd_ref, rows, act = refs[count + 2 :]
     width, half = w_dn.shape
     tokens = even_ref.shape[1]
-    views = [b.at[k] for b in blocks for k in range(b.shape[0])]
+    views = [b.at[k] for b, used in zip(blocks, counts) for k in range(used)]
     for k, view in enumerate(views):
         rows[pl.ds(k * tokens, tokens), :] = view[...]
     tail = rows[:, width : width + 2 * experts].astype(jnp.float32)
@@ -125,16 +126,23 @@
     ).astype(jnp.bfloat16)
     for k in range(len(views)):
         ref = (even_ref, odd_ref)[2 * k // len(views)]
-        ref[k % ref.shape[0]] = out[k * tokens : (k + 1) * tokens]
-
-
-def mlp(blocks, mine, mark, w_up, w_dn, experts):
-    count, number, tokens = len(blocks), sum(b.shape[0] for b in blocks), blocks[0].shape[1]
+        part = out[k * tokens : (k + 1) * tokens]
+        if ref.shape[2] > width:
+            filler = jnp.zeros((tokens, ref.shape[2] - width), part.dtype)
+            part = jnp.concatenate([part, filler], axis=1)
+        ref[k % ref.shape[0]] = part
+
+
+def mlp(blocks, counts, odd_width, mine, mark, w_up, w_dn, experts):
+    count, number, tokens = len(blocks), sum(counts), blocks[0].shape[1]
     m = number * tokens
     width, half = w_dn.shape
     return pl.pallas_call(
-        functools.partial(mlp_kernel, experts, count),
-        out_shape=[jax.ShapeDtypeStruct((number // 2, tokens, width), jnp.bfloat16)] * 2,
+        functools.partial(mlp_kernel, experts, counts),
+        out_shape=[
+            jax.ShapeDtypeStruct((number // 2, tokens, columns), jnp.bfloat16)
+            for columns in (width, odd_width)
+        ],
         in_specs=[SMEM, pl.BlockSpec(memory_space=pl.ANY)] + [VMEM] * (count + 2),
         out_specs=[VMEM] * 2,
         scratch_shapes=[
@@ -167,8 +175,11 @@
     experts = n // 2
     mine = lax.div(lax.axis_index("expert"), 2).reshape(1)
     own = pack(mine, residual, norm_gain, expert_ids, route_logits, experts)
-    def terms(mixed, other):
-        return mlp([mixed, other], mine, mark, w_up, w_dn, experts)
+    width = residual.shape[1]
+
+    def terms(mixed, other, odd_width=width):
+        counts = (mixed.shape[0],) * 2
+        return mlp([mixed, other], counts, odd_width, mine, mark, w_up, w_dn, experts)
 
     w_dn, mark = load(own, w_down[0].T)
     if n == 16:
@@ -184,30 +195,33 @@
         mixed = jnp.stack((own, side, near, near_side))
         mixed, far = together((mixed, far))
         far_side = swap(far, 2)
-        even, odd = terms(mixed, swap(mixed, 1))
+        even, odd = terms(mixed, swap(mixed, 1), own.shape[1])
         last, far_side, even = together((last, far_side, even))
         last_side = swap(last, 2)
         far_mixed = jnp.stack((far, far_side))
-        far_other = swap(far_mixed, 1)
-        first = add(even, swap(odd, 1))
+        far_other = swap(jnp.concatenate((far_mixed, odd)), 1)
+        first = add(even, far_other[2:, :, :width])
         far_even, far_odd = terms(far_mixed, far_other)
         last_side, far_even = together((last_side, far_even))
         last_mixed = jnp.stack((last, last_side))
         last_other = swap(last_mixed, 1)
         far_sums = add(far_even, swap(far_odd, 1))
         far_send = far_sums[1]
-        crossed = swap(first[2:], 4)
+        crossed = swap(first[3], 4)
         last_even, last_odd = terms(last_mixed, last_other)
         last_sums = add(last_even, swap(last_odd, 1))
         last_send = last_sums[1]
         far_away = swap(far_send, 2)
         last_away = swap(last_send, 2)
+        far_away, crossed = together((far_away, crossed))
         relayed = swap(add(far_sums[0], far_away), 4)
+        own_send = add(first[1], crossed)
+        own_send, last_away = together((own_send, last_away))
+        own_away = swap(own_send, 2)
         joined = add(last_sums[0], last_away, relayed)
-        own_send = add(first[1], crossed[1])
-        own_away = swap(own_send, 2)
+        near_back = swap(first[2], 4)
         last_back = swap(joined, 12)
-        return add(residual, first[0], crossed[0], own_away, last_back)
+        return add(residual, first[0], near_back, own_away, last_back)
     w_up, mark = load(mark, w_gate_up[0])
     blocks = {0: own}
     mask = n // 2

time: 60 us -> 58 us (0.967); the launches traced: 58.9 us -> 57.8 us
  waiting for transfers between devices: 15 us -> 14 us
    ppermute x19, waiting for transfers between devices: 15 us -> 14 us  [swap(): return lax.ppermute(x, 'expert', [(i, i ^ mask) for i in range(n)])]
  transfers between devices with their start and end apart: 19 -> 19, of which waited for: 9 -> 10; matrix products, arithmetic and copies ran while one was open for 1% -> 1% of each run, Pallas kernels for 26% -> 27%
where the time goes in v4:
time: 58 us; the launch traced here: 57.8 us
  starting transfers between devices  25.5 us (44%)
  Pallas kernels  16.5 us (28%)
  waiting for transfers between devices  14 us (24%)
  other arithmetic  1.64 us (3%)
    ppermute x19, starting transfers between devices, swap(): return lax.ppermute(x, 'expert', [(i, i ^ mask) for i in range(n)])  25.5 us
    ppermute x19, waiting for transfers between devices, swap(): return lax.ppermute(x, 'expert', [(i, i ^ mask) for i in range(n)])  14 us
    pallas_call x3, Pallas kernels, mlp(): pl.pallas_call(functools.partial(mlp_kernel, experts, counts), out_shape=...  9.58 us
    pallas_call x2, Pallas kernels, load(): pl.pallas_call(load_kernel, out_shape=[pltpu.VMEM(weight.shape, weight.dt...  5.78 us
    convert_element_type x7, other arithmetic, add(): return total.astype(jnp.bfloat16)  1.32 us
  transfers between devices with their start and end apart: 19, of which 10 were waited for; matrix products, arithmetic and copies ran while one was open for 1% of the time, Pallas kernels for 27%

profile of v4, /device:TPU:0, one launch (start us, length us, event | category | flops | bytes accessed | tf_op | source)
XLA Modules:
  0.0 57.8 jit_solution(8984652595900150711)
XLA Ops:
  0.0 1.1 %pack.1.refs_1_ = bf16[32,2944]{1,0:T(8,128)(2,1)S(1)} custom-call(s32[1]{0:T(128)} %bitcast._.mine_ref, bf16[32,2880]{1,0:T(8,128)(2,1)} %residual_hbm.1, f32[2880]{0:T(1024)} %gain_hbm.1, s32[4,32]{1,0:T(4,128)} %bitcast.55, f32[4,32]{1,0:T(4,128)} %bitcast.56), custom_call_target="tpu_custom_call" | custom-call | tf_op jit(solution)/shard_map/pack/pallas_call | solution.py:61
  1.2 3.1 %collective-permute-start.1 = (bf16[32,2944]{1,0:T(8,128)(2,1)S(1)}, bf16[32,2944]{1,0:T(8,128)(2,1)S(1)}, u32[]{:S(2)}, u32[]{:S(2)}) collective-permute-start(bf16[32,2944]{1,0:T(8,128)(2,1)S(1)} %pack.1.refs_1_), channel_id=1, source_target_pairs={{0,4},{1,5},{2,6},{3,7},{4,0},{5,1},{6,2},{7,3},{8,12},{9,13},{10,... | collective-permute-start | bytes 565256 | tf_op jit(solution)/shard_map/ppermute | solution.py:162
  4.2 1.5 %collective-permute-start.2 = (bf16[32,2944]{1,0:T(8,128)(2,1)S(1)}, bf16[32,2944]{1,0:T(8,128)(2,1)S(1)}, u32[]{:S(2)}, u32[]{:S(2)}) collective-permute-start(bf16[32,2944]{1,0:T(8,128)(2,1)S(1)} %pack.1.refs_1_), channel_id=1, source_target_pairs={{0,2},{1,3},{2,0},{3,1},{4,6},{5,7},{6,4},{7,5},{8,10},{9,11},{10,... | collective-permute-start | bytes 565256 | tf_op jit(solution)/shard_map/ppermute | solution.py:162
  5.8 2.6 %collective-permute-start = (bf16[32,2944]{1,0:T(8,128)(2,1)S(1)}, bf16[32,2944]{1,0:T(8,128)(2,1)S(1)}, u32[]{:S(2)}, u32[]{:S(2)}) collective-permute-start(bf16[32,2944]{1,0:T(8,128)(2,1)S(1)} %pack.1.refs_1_), channel_id=1, source_target_pairs={{0,8},{1,9},{2,10},{3,11},{4,12},{5,13},{6,14},{7,15},{8,0},{9,1},... | collective-permute-start | bytes 565256 | tf_op jit(solution)/shard_map/ppermute | solution.py:162
  8.4 2.3 %load.2 = (bf16[2880,768]{1,0:T(8,128)(2,1)S(1)}, f32[8,128]{1,0:T(8,128)S(1)}) custom-call(bf16[2880,768]{1,0:T(8,128)(2,1)} %bitcast.45, bf16[32,2944]{1,0:T(8,128)(2,1)S(1)} %pack.1.refs_1_), custom_call_target="tpu_custom_call" | custom-call | bytes 4423680 | tf_op jit(solution)/shard_map/load/pallas_call | solution.py:87
  10.8 3.6 %collective-permute-start.4 = (bf16[32,2944]{1,0:T(8,128)(2,1)S(1)}, bf16[32,2944]{1,0:T(8,128)(2,1)S(1)}, u32[]{:S(2)}, u32[]{:S(2)}) collective-permute-start(bf16[32,2944]{1,0:T(8,128)(2,1)S(1)} %collective-permute-done.1), channel_id=1, source_target_pairs={{0,2},{1,3},{2,0},{3,1},{4,6},{5,7},{6,4},{7,5},{8,10},{9,11},{10,... | collective-permute-start | bytes 565256 | tf_op jit(solution)/shard_map/ppermute | solution.py:162
  14.4 3.5 %load.3 = (bf16[2880,1536]{1,0:T(8,128)(2,1)S(1)}, f32[8,128]{1,0:T(8,128)S(1)}) custom-call(bf16[2880,1536]{1,0:T(8,128)(2,1)} %bitcast.44, f32[8,128]{1,0:T(8,128)S(1)} %get-tuple-element.32.refs_1_), custom_call_target="tpu_custom_call" | custom-call | bytes 8847360 | tf_op jit(solution)/shard_map/load/pallas_call | solution.py:87
  18.2 2.1 %collective-permute-start.5 = (bf16[32,2944]{1,0:T(8,128)(2,1)S(1)}, bf16[32,2944]{1,0:T(8,128)(2,1)S(1)}, u32[]{:S(2)}, u32[]{:S(2)}) collective-permute-start(bf16[32,2944]{1,0:T(8,128)(2,1)S(1)} %collective-permute-done), channel_id=1, source_target_pairs={{0,2},{1,3},{2,0},{3,1},{4,6},{5,7},{6,4},{7,5},{8,10},{9,11},{10,... | collective-permute-start | bytes 565256 | tf_op jit(solution)/shard_map/ppermute | solution.py:162
  20.3 3.9 %mlp.3 = (bf16[4,32,2880]{2,1,0:T(8,128)(2,1)S(1)}, bf16[4,32,2944]{2,1,0:T(8,128)(2,1)S(1)}) custom-call(s32[1]{0:T(128)} %bitcast._.mine_ref, f32[8,128]{1,0:T(8,128)S(1)} %get-tuple-element.38.mark_ref, bf16[4,32,2944]{2,1,0:T(8,128)(2,1)S(1)} %pad_maximum_fusion.1.refs_0_, bf16[4,32,2944]{2,1,0:T(8,128)(2,1)S(1)} %collective-permute-done.6.refs_1_, ...), custom_call_target="tpu_custom_call" | custom-call | flops 3397386240 | bytes 13271040 | tf_op jit(solution)/shard_map/mlp/pallas_call | solution.py:140
  24.2 1.0 %collective-permute-done.3 = bf16[32,2944]{1,0:T(8,128)(2,1)S(1)} collective-permute-done((bf16[32,2944]{1,0:T(8,128)(2,1)S(1)}, bf16[32,2944]{1,0:T(8,128)(2,1)S(1)}, u32[]{:S(2)}, u32[]{:S(2)}) %collective-permute-start.3) | collective-permute-done | bytes 188448 | tf_op jit(solution)/shard_map/ppermute | solution.py:162
  25.7 1.8 %collective-permute-start.9 = (bf16[32,2944]{1,0:T(8,128)(2,1)S(1)}, bf16[32,2944]{1,0:T(8,128)(2,1)S(1)}, u32[]{:S(2)}, u32[]{:S(2)}) collective-permute-start(bf16[32,2944]{1,0:T(8,128)(2,1)S(1)} %collective-permute-done.3), channel_id=1, source_target_pairs={{0,2},{1,3},{2,0},{3,1},{4,6},{5,7},{6,4},{7,5},{8,10},{9,11},{10,... | collective-permute-start | bytes 565256 | tf_op jit(solution)/shard_map/ppermute | solution.py:162
  27.6 0.9 %collective-permute-done.7.refs_1_ = bf16[6,32,2944]{2,1,0:T(8,128)(2,1)S(1)} collective-permute-done((bf16[6,32,2944]{2,1,0:T(8,128)(2,1)S(1)}, bf16[6,32,2944]{2,1,0:T(8,128)(2,1)S(1)}, u32[]{:S(2)}, u32[]{:S(2)}) %collective-permute-start.7) | collective-permute-done | bytes 1130528 | tf_op jit(solution)/shard_map/ppermute | solution.py:162
  28.5 2.9 %mlp.4 = (bf16[2,32,2880]{2,1,0:T(8,128)(2,1)S(1)}, bf16[2,32,2880]{2,1,0:T(8,128)(2,1)S(1)}) custom-call(s32[1]{0:T(128)} %bitcast._.mine_ref, f32[8,128]{1,0:T(8,128)S(1)} %get-tuple-element.38.mark_ref, bf16[2,32,2944]{2,1,0:T(8,128)(2,1)S(1)} %pad_maximum_fusion.2.refs_0_, bf16[6,32,2944]{2,1,0:T(8,128)(2,1)S(1)} %collective-permute-done.7.refs_1_, ...), custom_call_target="tpu_custom_call" | custom-call | flops 1698693120 | bytes 13271040 | tf_op jit(solution)/shard_map/mlp/pallas_call | solution.py:140
  31.8 1.1 %collective-permute-done.9 = bf16[32,2944]{1,0:T(8,128)(2,1)S(1)} collective-permute-done((bf16[32,2944]{1,0:T(8,128)(2,1)S(1)}, bf16[32,2944]{1,0:T(8,128)(2,1)S(1)}, u32[]{:S(2)}, u32[]{:S(2)}) %collective-permute-start.9) | collective-permute-done | bytes 188448 | tf_op jit(solution)/shard_map/ppermute | solution.py:162
  32.9 1.8 %collective-permute-start.12 = (bf16[32,2880]{1,0:T(8,128)(2,1)S(1)}, bf16[32,2880]{1,0:T(8,128)(2,1)S(1)}, u32[]{:S(2)}, u32[]{:S(2)}) collective-permute-start(bf16[32,2880]{1,0:T(8,128)(2,1)S(1)} %get-tuple-element.58), channel_id=1, source_target_pairs={{0,4},{1,5},{2,6},{3,7},{4,0},{5,1},{6,2},{7,3},{8,12},{9,13},{10,... | collective-permute-start | bytes 552968 | tf_op jit(solution)/shard_map/ppermute | solution.py:162
  34.9 1.8 %collective-permute-start.11 = (bf16[32,2880]{1,0:T(8,128)(2,1)S(1)}, bf16[32,2880]{1,0:T(8,128)(2,1)S(1)}, u32[]{:S(2)}, u32[]{:S(2)}) collective-permute-start(bf16[32,2880]{1,0:T(8,128)(2,1)S(1)} %slice_bitcast_fusion.4), channel_id=1, source_target_pairs={{0,2},{1,3},{2,0},{3,1},{4,6},{5,7},{6,4},{7,5},{8,10},{9,11},{10,... | collective-permute-start | bytes 552968 | tf_op jit(solution)/shard_map/ppermute | solution.py:162
  37.0 2.8 %mlp.5 = (bf16[2,32,2880]{2,1,0:T(8,128)(2,1)S(1)}, bf16[2,32,2880]{2,1,0:T(8,128)(2,1)S(1)}) custom-call(s32[1]{0:T(128)} %bitcast._.mine_ref, f32[8,128]{1,0:T(8,128)S(1)} %get-tuple-element.38.mark_ref, bf16[2,32,2944]{2,1,0:T(8,128)(2,1)S(1)} %pad_maximum_fusion.3.refs_0_, bf16[2,32,2944]{2,1,0:T(8,128)(2,1)S(1)} %collective-permute-done.13.refs_1_, ...), custom_call_target="tpu_custom_call" | custom-call | flops 1698693120 | bytes 13271040 | tf_op jit(solution)/shard_map/mlp/pallas_call | solution.py:140
  39.9 2.2 %collective-permute-done.11 = bf16[32,2880]{1,0:T(8,128)(2,1)S(1)} collective-permute-done((bf16[32,2880]{1,0:T(8,128)(2,1)S(1)}, bf16[32,2880]{1,0:T(8,128)(2,1)S(1)}, u32[]{:S(2)}, u32[]{:S(2)}) %collective-permute-start.11) | collective-permute-done | bytes 184352 | tf_op jit(solution)/shard_map/ppermute | solution.py:162
  42.6 1.8 %collective-permute-start.15 = (bf16[32,2880]{1,0:T(8,128)(2,1)S(1)}, bf16[32,2880]{1,0:T(8,128)(2,1)S(1)}, u32[]{:S(2)}, u32[]{:S(2)}) collective-permute-start(bf16[32,2880]{1,0:T(8,128)(2,1)S(1)} %slice_bitcast_fusion.2), channel_id=1, source_target_pairs={{0,2},{1,3},{2,0},{3,1},{4,6},{5,7},{6,4},{7,5},{8,10},{9,11},{10,... | collective-permute-start | bytes 552968 | tf_op jit(solution)/shard_map/ppermute | solution.py:162
  44.4 4.4 %collective-permute-done.15 = bf16[32,2880]{1,0:T(8,128)(2,1)S(1)} collective-permute-done((bf16[32,2880]{1,0:T(8,128)(2,1)S(1)}, bf16[32,2880]{1,0:T(8,128)(2,1)S(1)}, u32[]{:S(2)}, u32[]{:S(2)}) %collective-permute-start.15) | collective-permute-done | bytes 184352 | tf_op jit(solution)/shard_map/ppermute | solution.py:162
  48.9 2.5 %collective-permute-start.18 = (bf16[32,2880]{1,0:T(8,128)(2,1)S(1)}, bf16[32,2880]{1,0:T(8,128)(2,1)S(1)}, u32[]{:S(2)}, u32[]{:S(2)}) collective-permute-start(bf16[32,2880]{1,0:T(8,128)(2,1)S(1)} %fusion.2), channel_id=1, source_target_pairs={{0,12},{1,13},{2,14},{3,15},{4,8},{5,9},{6,10},{7,11},{8,4},{9,5},... | collective-permute-start | bytes 552968 | tf_op jit(solution)/shard_map/ppermute | solution.py:162
  51.4 1.7 %collective-permute-start.16 = (bf16[32,2880]{1,0:T(8,128)(2,1)S(1)}, bf16[32,2880]{1,0:T(8,128)(2,1)S(1)}, u32[]{:S(2)}, u32[]{:S(2)}) collective-permute-start(bf16[32,2880]{1,0:T(8,128)(2,1)S(1)} %fusion.3), channel_id=1, source_target_pairs={{0,2},{1,3},{2,0},{3,1},{4,6},{5,7},{6,4},{7,5},{8,10},{9,11},{10,... | collective-permute-start | bytes 552968 | tf_op jit(solution)/shard_map/ppermute | solution.py:162
  53.1 3.3 %collective-permute-done.18 = bf16[32,2880]{1,0:T(8,128)(2,1)S(1)} collective-permute-done((bf16[32,2880]{1,0:T(8,128)(2,1)S(1)}, bf16[32,2880]{1,0:T(8,128)(2,1)S(1)}, u32[]{:S(2)}, u32[]{:S(2)}) %collective-permute-start.18) | collective-permute-done | bytes 184352 | tf_op jit(solution)/shard_map/ppermute | solution.py:162
  57.0 0.8 %fusion.7 = bf16[32,2880]{1,0:T(8,128)(2,1)} fusion(bf16[32,2880]{1,0:T(8,128)(2,1)S(1)} %collective-permute-done.18, bf16[32,2880]{1,0:T(8,128)(2,1)S(1)} %collective-permute-done.16, bf16[32,2880]{1,0:T(8,128)(2,1)S(1)} %collective-permute-done.8, bf16[32,2880]{1,0:T(8,128)(2,1)S(1)} %copy-done, bf16[4,32,2880]{2,1,0:T(8,128)(2,1)S(1)} %add_convert_fusion), kind=kLoop, calls=%fused_computation.18 | loop fusion | flops 921600 | bytes 1105920 | tf_op jit(solution)/shard_map/convert_element_type | solution.py:169
  (36 shorter events, 3.3 us)
Async XLA Ops:
  1.2 9.6 %collective-permute-start.1 = (bf16[32,2944]{1,0:T(8,128)(2,1)S(1)}, bf16[32,2944]{1,0:T(8,128)(2,1)S(1)}, u32[]{:S(2)}, u32[]{:S(2)}) collective-permute-start(bf16[32,2944]{1,0:T(8,128)(2,1)S(1)} %pack.1.refs_1_), channel_id=1, source_target_pairs={{0,4},{1,5},{2,6},{3,7},{4,0},{5,1},{6,2},{7,3},{8,12},{9,13},{10,... | collective-permute-start | bytes 565256 | tf_op jit(solution)/shard_map/ppermute | solution.py:162
  4.2 6.5 %collective-permute-start.2 = (bf16[32,2944]{1,0:T(8,128)(2,1)S(1)}, bf16[32,2944]{1,0:T(8,128)(2,1)S(1)}, u32[]{:S(2)}, u32[]{:S(2)}) collective-permute-start(bf16[32,2944]{1,0:T(8,128)(2,1)S(1)} %pack.1.refs_1_), channel_id=1, source_target_pairs={{0,2},{1,3},{2,0},{3,1},{4,6},{5,7},{6,4},{7,5},{8,10},{9,11},{10,... | collective-permute-start | bytes 565256 | tf_op jit(solution)/shard_map/ppermute | solution.py:162
  5.8 12.1 %collective-permute-start = (bf16[32,2944]{1,0:T(8,128)(2,1)S(1)}, bf16[32,2944]{1,0:T(8,128)(2,1)S(1)}, u32[]{:S(2)}, u32[]{:S(2)}) collective-permute-start(bf16[32,2944]{1,0:T(8,128)(2,1)S(1)} %pack.1.refs_1_), channel_id=1, source_target_pairs={{0,8},{1,9},{2,10},{3,11},{4,12},{5,13},{6,14},{7,15},{8,0},{9,1},... | collective-permute-start | bytes 565256 | tf_op jit(solution)/shard_map/ppermute | solution.py:162
  10.8 7.1 %collective-permute-start.4 = (bf16[32,2944]{1,0:T(8,128)(2,1)S(1)}, bf16[32,2944]{1,0:T(8,128)(2,1)S(1)}, u32[]{:S(2)}, u32[]{:S(2)}) collective-permute-start(bf16[32,2944]{1,0:T(8,128)(2,1)S(1)} %collective-permute-done.1), channel_id=1, source_target_pairs={{0,2},{1,3},{2,0},{3,1},{4,6},{5,7},{6,4},{7,5},{8,10},{9,11},{10,... | collective-permute-start | bytes 565256 | tf_op jit(solution)/shard_map/ppermute | solution.py:162
  18.0 2.3 %collective-permute-start.6 = (bf16[4,32,2944]{2,1,0:T(8,128)(2,1)S(1)}, bf16[4,32,2944]{2,1,0:T(8,128)(2,1)S(1)}, u32[]{:S(2)}, u32[]{:S(2)}) collective-permute-start(bf16[4,32,2944]{2,1,0:T(8,128)(2,1)S(1)} %pad_maximum_fusion.1.refs_0_), channel_id=1, source_target_pairs={{0,1},{1,0},{2,3},{3,2},{4,5},{5,4},{6,7},{7,6},{8,9},{9,8},{10,11... | collective-permute-start | bytes 2261000 | tf_op jit(solution)/shard_map/ppermute | solution.py:162
  18.1 7.1 %collective-permute-start.3 = (bf16[32,2944]{1,0:T(8,128)(2,1)S(1)}, bf16[32,2944]{1,0:T(8,128)(2,1)S(1)}, u32[]{:S(2)}, u32[]{:S(2)}) collective-permute-start(bf16[32,2944]{1,0:T(8,128)(2,1)S(1)} %collective-permute-done), channel_id=1, source_target_pairs={{0,4},{1,5},{2,6},{3,7},{4,0},{5,1},{6,2},{7,3},{8,12},{9,13},{10,... | collective-permute-start | bytes 565256 | tf_op jit(solution)/shard_map/ppermute | solution.py:162
  18.2 7.3 %collective-permute-start.5 = (bf16[32,2944]{1,0:T(8,128)(2,1)S(1)}, bf16[32,2944]{1,0:T(8,128)(2,1)S(1)}, u32[]{:S(2)}, u32[]{:S(2)}) collective-permute-start(bf16[32,2944]{1,0:T(8,128)(2,1)S(1)} %collective-permute-done), channel_id=1, source_target_pairs={{0,2},{1,3},{2,0},{3,1},{4,6},{5,7},{6,4},{7,5},{8,10},{9,11},{10,... | collective-permute-start | bytes 565256 | tf_op jit(solution)/shard_map/ppermute | solution.py:162
  25.6 2.8 %collective-permute-start.7 = (bf16[6,32,2944]{2,1,0:T(8,128)(2,1)S(1)}, bf16[6,32,2944]{2,1,0:T(8,128)(2,1)S(1)}, u32[]{:S(2)}, u32[]{:S(2)}) collective-permute-start(bf16[6,32,2944]{2,1,0:T(8,128)(2,1)S(1)} %pad_maximum_fusion), channel_id=1, source_target_pairs={{0,1},{1,0},{2,3},{3,2},{4,5},{5,4},{6,7},{7,6},{8,9},{9,8},{10,11... | collective-permute-start | bytes 3391496 | tf_op jit(solution)/shard_map/ppermute | solution.py:162
  25.7 7.1 %collective-permute-start.9 = (bf16[32,2944]{1,0:T(8,128)(2,1)S(1)}, bf16[32,2944]{1,0:T(8,128)(2,1)S(1)}, u32[]{:S(2)}, u32[]{:S(2)}) collective-permute-start(bf16[32,2944]{1,0:T(8,128)(2,1)S(1)} %collective-permute-done.3), channel_id=1, source_target_pairs={{0,2},{1,3},{2,0},{3,1},{4,6},{5,7},{6,4},{7,5},{8,10},{9,11},{10,... | collective-permute-start | bytes 565256 | tf_op jit(solution)/shard_map/ppermute | solution.py:162
  31.4 3.4 %collective-permute-start.10 = (bf16[2,32,2880]{2,1,0:T(8,128)(2,1)S(1)}, bf16[2,32,2880]{2,1,0:T(8,128)(2,1)S(1)}, u32[]{:S(2)}, u32[]{:S(2)}) collective-permute-start(bf16[2,32,2880]{2,1,0:T(8,128)(2,1)S(1)} %get-tuple-element.49), channel_id=1, source_target_pairs={{0,1},{1,0},{2,3},{3,2},{4,5},{5,4},{6,7},{7,6},{8,9},{9,8},{10,11... | collective-permute-start | bytes 1105928 | tf_op jit(solution)/shard_map/ppermute | solution.py:162
  32.9 7.0 %collective-permute-start.12 = (bf16[32,2880]{1,0:T(8,128)(2,1)S(1)}, bf16[32,2880]{1,0:T(8,128)(2,1)S(1)}, u32[]{:S(2)}, u32[]{:S(2)}) collective-permute-start(bf16[32,2880]{1,0:T(8,128)(2,1)S(1)} %get-tuple-element.58), channel_id=1, source_target_pairs={{0,4},{1,5},{2,6},{3,7},{4,0},{5,1},{6,2},{7,3},{8,12},{9,13},{10,... | collective-permute-start | bytes 552968 | tf_op jit(solution)/shard_map/ppermute | solution.py:162
  34.7 2.3 %collective-permute-start.13 = (bf16[2,32,2944]{2,1,0:T(8,128)(2,1)S(1)}, bf16[2,32,2944]{2,1,0:T(8,128)(2,1)S(1)}, u32[]{:S(2)}, u32[]{:S(2)}) collective-permute-start(bf16[2,32,2944]{2,1,0:T(8,128)(2,1)S(1)} %pad_maximum_fusion.3.refs_0_), channel_id=1, source_target_pairs={{0,1},{1,0},{2,3},{3,2},{4,5},{5,4},{6,7},{7,6},{8,9},{9,8},{10,11... | collective-permute-start | bytes 1130504 | tf_op jit(solution)/shard_map/ppermute | solution.py:162
  34.9 7.2 %collective-permute-start.11 = (bf16[32,2880]{1,0:T(8,128)(2,1)S(1)}, bf16[32,2880]{1,0:T(8,128)(2,1)S(1)}, u32[]{:S(2)}, u32[]{:S(2)}) collective-permute-start(bf16[32,2880]{1,0:T(8,128)(2,1)S(1)} %slice_bitcast_fusion.4), channel_id=1, source_target_pairs={{0,2},{1,3},{2,0},{3,1},{4,6},{5,7},{6,4},{7,5},{8,10},{9,11},{10,... | collective-permute-start | bytes 552968 | tf_op jit(solution)/shard_map/ppermute | solution.py:162
  36.7 16.4 %collective-permute-start.8 = (bf16[32,2880]{1,0:T(8,128)(2,1)S(1)}, bf16[32,2880]{1,0:T(8,128)(2,1)S(1)}, u32[]{:S(2)}, u32[]{:S(2)}) collective-permute-start(bf16[32,2880]{1,0:T(8,128)(2,1)S(1)} %get-tuple-element.57), channel_id=1, source_target_pairs={{0,4},{1,5},{2,6},{3,7},{4,0},{5,1},{6,2},{7,3},{8,12},{9,13},{10,... | collective-permute-start | bytes 552968 | tf_op jit(solution)/shard_map/ppermute | solution.py:162
  39.8 2.7 %collective-permute-start.14 = (bf16[2,32,2880]{2,1,0:T(8,128)(2,1)S(1)}, bf16[2,32,2880]{2,1,0:T(8,128)(2,1)S(1)}, u32[]{:S(2)}, u32[]{:S(2)}) collective-permute-start(bf16[2,32,2880]{2,1,0:T(8,128)(2,1)S(1)} %get-tuple-element.53), channel_id=1, source_target_pairs={{0,1},{1,0},{2,3},{3,2},{4,5},{5,4},{6,7},{7,6},{8,9},{9,8},{10,11... | collective-permute-start | bytes 1105928 | tf_op jit(solution)/shard_map/ppermute | solution.py:162
  42.1 6.7 %collective-permute-start.17 = (bf16[32,2880]{1,0:T(8,128)(2,1)S(1)}, bf16[32,2880]{1,0:T(8,128)(2,1)S(1)}, u32[]{:S(2)}, u32[]{:S(2)}) collective-permute-start(bf16[32,2880]{1,0:T(8,128)(2,1)S(1)} %fusion), channel_id=1, source_target_pairs={{0,4},{1,5},{2,6},{3,7},{4,0},{5,1},{6,2},{7,3},{8,12},{9,13},{10,... | collective-permute-start | bytes 552968 | tf_op jit(solution)/shard_map/ppermute | solution.py:162
  42.5 14.5 %copy-start = (bf16[32,2880]{1,0:T(8,128)(2,1)S(1)}, bf16[32,2880]{1,0:T(8,128)(2,1)}, u32[]{:S(2)}) copy-start(bf16[32,2880]{1,0:T(8,128)(2,1)} %residual_hbm.1) | copy-start | bytes 552964
  42.6 6.2 %collective-permute-start.15 = (bf16[32,2880]{1,0:T(8,128)(2,1)S(1)}, bf16[32,2880]{1,0:T(8,128)(2,1)S(1)}, u32[]{:S(2)}, u32[]{:S(2)}) collective-permute-start(bf16[32,2880]{1,0:T(8,128)(2,1)S(1)} %slice_bitcast_fusion.2), channel_id=1, source_target_pairs={{0,2},{1,3},{2,0},{3,1},{4,6},{5,7},{6,4},{7,5},{8,10},{9,11},{10,... | collective-permute-start | bytes 552968 | tf_op jit(solution)/shard_map/ppermute | solution.py:162
  48.9 7.5 %collective-permute-start.18 = (bf16[32,2880]{1,0:T(8,128)(2,1)S(1)}, bf16[32,2880]{1,0:T(8,128)(2,1)S(1)}, u32[]{:S(2)}, u32[]{:S(2)}) collective-permute-start(bf16[32,2880]{1,0:T(8,128)(2,1)S(1)} %fusion.2), channel_id=1, source_target_pairs={{0,12},{1,13},{2,14},{3,15},{4,8},{5,9},{6,10},{7,11},{8,4},{9,5},... | collective-permute-start | bytes 552968 | tf_op jit(solution)/shard_map/ppermute | solution.py:162
  51.4 5.6 %collective-permute-start.16 = (bf16[32,2880]{1,0:T(8,128)(2,1)S(1)}, bf16[32,2880]{1,0:T(8,128)(2,1)S(1)}, u32[]{:S(2)}, u32[]{:S(2)}) collective-permute-start(bf16[32,2880]{1,0:T(8,128)(2,1)S(1)} %fusion.3), channel_id=1, source_target_pairs={{0,2},{1,3},{2,0},{3,1},{4,6},{5,7},{6,4},{7,5},{8,10},{9,11},{10,... | collective-permute-start | bytes 552968 | tf_op jit(solution)/shard_map/ppermute | solution.py:162
